TPU v7x, 32 devices: a whole 2x2x4 slice. The times are simulated.
32 devices in a mesh: tr: 4 (over x, core), gz: 8 (over z, y).
Axes of the slice: x: 2, y: 2, z: 4, core: 2. Of those that a mesh axis runs over, the one named last changes fastest.
Arguments:
- tokens: bfloat16 [40, 32, 8, 768], P('gz', None, 'tr'), may hold values from -6 to 6
- cotangent: bfloat16 [40, 32, 8, 768], P('gz', None, 'tr'), may hold values from -6 to 6
- gain_x: float32 [768], replicated, may hold values from 0.1 to 1.9
- wqkv_x: bfloat16 [768, 2304], P('tr'), as said below
- wo_x: bfloat16 [768, 768], P('tr'), may hold values from -0.21875 to 0.21875
- gain_z: float32 [768], replicated, may hold values from 0.1 to 1.9
- wqkv_z: bfloat16 [768, 2304], P('tr'), as said below
- wo_z: bfloat16 [768, 768], P('tr'), may hold values from -0.21875 to 0.21875
Outputs:
- grad_tokens: bfloat16 [40, 32, 8, 768], P('gz', None, 'tr')
Inputs may be any that keep to these rules, and one draw needn't show every extreme that they name: `wqkv_x`: query, key and value columns side by side, each block split into 6 heads of 128. `wqkv_z`: query, key and value columns side by side, each block split into 6 heads of 128.
All inputs are finite; a program needn't handle non-finite values.
Results may differ from a plain program's by a relative error of at most 0.038.
The roundings to bfloat16 on the way count: a program that leaves them out, or rounds other values in their place, can miss the bound.
Values may be sent and summed in bfloat16 or wider, within the bound.
A program may use at most 64 MiB of HBM per device.

v0:
```python
import math

import jax
import jax.numpy as jnp
from jax import lax
from jax.sharding import PartitionSpec as P

H = 6


def head_split(packed, index, model_width):
    piece = packed[..., index * model_width : (index + 1) * model_width]
    return piece.reshape(piece.shape[:-1] + (H, model_width // H))


def merge_heads(value):
    return value.reshape(value.shape[:-2] + (value.shape[-2] * value.shape[-1],))


def recompute(tokens_in, gain_vec, w_in, layout):
    model_width = w_in.shape[0]
    factor = 1.0 / math.sqrt(model_width // H)
    widened = tokens_in.astype(jnp.float32)
    inv_rms = lax.rsqrt(jnp.mean(widened * widened, axis=-1, keepdims=True) + 1e-06)
    normed = (widened * inv_rms * gain_vec).astype(jnp.bfloat16)
    packed = jnp.dot(normed, w_in, preferred_element_type=jnp.float32).astype(jnp.bfloat16)
    queries = head_split(packed, 0, model_width)
    key_part = head_split(packed, 1, model_width)
    values = head_split(packed, 2, model_width)
    key_form = layout.replace("l", "m")
    scores = (
        jnp.einsum(
            layout + "," + key_form + "->bhlm",
            queries,
            key_part,
            preferred_element_type=jnp.float32,
        )
        * factor
    )
    highest = jnp.max(scores, axis=-1, keepdims=True)
    expanded = jnp.exp(scores - highest)
    probs = expanded / jnp.sum(expanded, axis=-1, keepdims=True)
    return (widened, inv_rms, queries, key_part, values, probs, probs.astype(jnp.bfloat16), factor)


def forward_out(tokens_in, gain_vec, w_in, w_out, layout):
    widened, inv_rms, queries, key_part, values, probs, probs_b, factor = recompute(
        tokens_in, gain_vec, w_in, layout
    )
    key_form = layout.replace("l", "m")
    mixed = jnp.einsum(
        "bhlm," + key_form + "->" + layout, probs_b, values, preferred_element_type=jnp.float32
    )
    mixed = merge_heads(mixed.astype(jnp.bfloat16))
    return (widened + jnp.dot(mixed, w_out, preferred_element_type=jnp.float32)).astype(
        jnp.bfloat16
    )


def backward(tokens_in, upstream, gain_vec, w_in, w_out, layout):
    widened, inv_rms, queries, key_part, values, probs, probs_b, factor = recompute(
        tokens_in, gain_vec, w_in, layout
    )
    key_form = layout.replace("l", "m")
    d_mixed = jnp.dot(upstream, w_out.T, preferred_element_type=jnp.float32).astype(jnp.bfloat16)
    d_mixed = d_mixed.reshape(d_mixed.shape[:-1] + (H, d_mixed.shape[-1] // H))
    d_probs = jnp.einsum(
        layout + "," + key_form + "->bhlm", d_mixed, values, preferred_element_type=jnp.float32
    )
    d_values = jnp.einsum(
        "bhlm," + layout + "->" + key_form, probs_b, d_mixed, preferred_element_type=jnp.float32
    ).astype(jnp.bfloat16)
    centre = jnp.sum(probs * d_probs, axis=-1, keepdims=True)
    d_scores = (probs * (d_probs - centre) * factor).astype(jnp.bfloat16)
    d_queries = jnp.einsum(
        "bhlm," + key_form + "->" + layout, d_scores, key_part, preferred_element_type=jnp.float32
    ).astype(jnp.bfloat16)
    d_keys = jnp.einsum(
        "bhlm," + layout + "->" + key_form, d_scores, queries, preferred_element_type=jnp.float32
    ).astype(jnp.bfloat16)
    joined = jnp.concatenate(
        [merge_heads(d_queries), merge_heads(d_keys), merge_heads(d_values)], axis=-1
    )
    d_normed = jnp.dot(joined, w_in.T, preferred_element_type=jnp.float32)
    scaled = d_normed * gain_vec
    d_tokens = inv_rms * (
        scaled - widened * inv_rms * inv_rms * jnp.mean(scaled * widened, axis=-1, keepdims=True)
    )
    return (upstream.astype(jnp.float32) + d_tokens).astype(jnp.bfloat16)


def line_forward(lines, gain_vec, w_in, w_out):
    feature_count = lines.shape[3]
    flat = lines.reshape(-1, lines.shape[2], feature_count)
    return forward_out(flat, gain_vec, w_in, w_out, "blhe").reshape(lines.shape)


def line_backward(lines, upstream, gain_vec, w_in, w_out):
    feature_count = lines.shape[3]
    flat = lines.reshape(-1, lines.shape[2], feature_count)
    flat_up = upstream.reshape(flat.shape)
    return backward(flat, flat_up, gain_vec, w_in, w_out, "blhe").reshape(lines.shape)


def column_backward(columns, upstream, gain_vec, w_in, w_out):
    feature_count = columns.shape[3]
    flat = columns.reshape(columns.shape[0], -1, feature_count)
    flat_up = upstream.reshape(flat.shape)
    return backward(flat, flat_up, gain_vec, w_in, w_out, "lbhe").reshape(columns.shape)


def per_device(tokens, cotangent, gain_x, wqkv_x, wo_x, gain_z, wqkv_z, wo_z):
    full_in_x, full_out_x = (
        lax.all_gather(wqkv_x, "tr", axis=0, tiled=True),
        lax.all_gather(wo_x, "tr", axis=0, tiled=True),
    )
    full_in_z, full_out_z = (
        lax.all_gather(wqkv_z, "tr", axis=0, tiled=True),
        lax.all_gather(wo_z, "tr", axis=0, tiled=True),
    )
    lines = lax.all_to_all(tokens, "tr", split_axis=1, concat_axis=2, tiled=True)
    mid_lines = line_forward(lines, gain_x, full_in_x, full_out_x)
    mid_home = lax.all_to_all(mid_lines, "tr", split_axis=2, concat_axis=1, tiled=True)
    mid_columns, cot_columns = (
        lax.all_to_all(mid_home, "gz", split_axis=1, concat_axis=0, tiled=True),
        lax.all_to_all(cotangent, "gz", split_axis=1, concat_axis=0, tiled=True),
    )
    grad_columns = column_backward(mid_columns, cot_columns, gain_z, full_in_z, full_out_z)
    grad_home = lax.all_to_all(grad_columns, "gz", split_axis=0, concat_axis=1, tiled=True)
    grad_lines = lax.all_to_all(grad_home, "tr", split_axis=1, concat_axis=2, tiled=True)
    result_lines = line_backward(lines, grad_lines, gain_x, full_in_x, full_out_x)
    return lax.all_to_all(result_lines, "tr", split_axis=2, concat_axis=1, tiled=True)


def solution(mesh):
    return jax.shard_map(
        per_device,
        mesh=mesh,
        in_specs=(
            P("gz", None, "tr", None),
            P("gz", None, "tr", None),
            P(),
            P("tr", None),
            P("tr", None),
            P(),
            P("tr", None),
            P("tr", None),
        ),
        out_specs=P("gz", None, "tr", None),
        check_vma=False,
    )
```

profile of v0, /device:TPU:0, one launch (start us, length us, event | category | flops | bytes accessed | tf_op | source)
XLA Modules:
  0.0 204.5 jit_solution(4748375332950827207)
XLA Ops:
  6.5 0.7 all-gather.5.cloned.1.call-update
  7.3 0.7 all-gather.7.cloned.1.call-update
  8.1 0.7 all-gather.11.cloned.1.call-update
  8.8 0.5 all-gather.9.cloned.1.call-update
  9.7 13.0 %all_to_all.102 = bf16[5,32,2,768]{3,2,0,1:T(2,128)(2,1)S(1)} all-to-all(bf16[5,32,2,768]{3,2,0,1:T(2,128)(2,1)S(1)} %copy.148), channel_id=1, replica_groups=mesh['tr'=4,'gz'=8] {'tr'}, dimensions={1} | all-to-all | bytes 983040 | tf_op jit(solution)/shard_map/all_to_all | solution.py:121
  22.7 0.6 multiply_reduce_fusion.4
  23.6 0.4 copy_bitcast_fusion
  24.0 0.7 reshape.154
  24.7 18.0 %all-gather.5.cloned.1.call-done = bf16[768,2304]{1,0:T(8,128)(2,1)} async-done(((bf16[192,2304]{1,0:T(8,128)(2,1)}), bf16[768,2304]{1,0:T(8,128)(2,1)}) %all-gather.5.cloned.1.call-update) | async-done | bytes 3538960 | tf_op jit(solution)/shard_map/all_gather | solution.py:114
  42.7 3.4 %convolution_convert_fusion.1 = bf16[40,8,2304]{2,1,0:T(8,128)(2,1)S(1)} fusion(bf16[768,2304]{1,0:T(8,128)(2,1)} %all-gather.5.cloned.1.call-done, f32[40,8,768]{2,1,0:T(8,128)S(1)} %reshape.154, f32[768]{0:T(1024)S(1)} %copy-done.8, f32[40,8]{1,0:T(8,128)S(1)} %copy.153), kind=kOutput, calls=%fused_computation.5 | convolution fusion | flops 1133936640 | bytes 6000896 | tf_op jit(solution)/shard_map/dot_general | solution.py:26
  46.1 1.8 fusion.105
  47.9 14.2 %all-gather.7.cloned.1.call-done = bf16[768,768]{1,0:T(8,128)(2,1)} async-done(((bf16[192,768]{1,0:T(8,128)(2,1)}), bf16[768,768]{1,0:T(8,128)(2,1)}) %all-gather.7.cloned.1.call-update) | async-done | bytes 1179664 | tf_op jit(solution)/shard_map/all_gather | solution.py:115
  62.1 2.5 %fusion.40 = bf16[40,8,768]{2,1,0:T(8,128)(2,1)S(1)} fusion(f32[40,8,768]{2,1,0:T(8,128)S(1)} %reshape.154, bf16[768,768]{1,0:T(8,128)(2,1)} %all-gather.7.cloned.1.call-done, bf16[40,8,2304]{2,1,0:T(8,128)(2,1)S(1)} %convolution_convert_fusion.1, f32[40,6,8,8]{2,3,1,0:T(8,128)} %get-tuple-element.9, f32[40,6,8]{2,1,0:T(8,128)S(1)} %get-tuple-element.8), kind=kOutput, calls=%fused_computation.37 | convolution fusion | flops 382187520 | bytes 3371008 | tf_op jit(solution)/shard_map/dot_general | solution.py:55
  64.6 0.9 copy.155
  65.5 3.5 %all-to-all-start.2 = ((bf16[5,8,8,768]{3,1,0,2:T(8,128)(2,1)}), bf16[5,8,8,768]{3,1,0,2:T(8,128)(2,1)S(1)}, u32[]{:S(2)}, u32[]{:S(2)}) async-start(bf16[5,8,8,768]{3,1,0,2:T(8,128)(2,1)} %copy.155), calls=%async_computation.2 | async-start | bytes 983040 | tf_op jit(solution)/shard_map/all_to_all | solution.py:123
  69.0 1.1 copy.146
  70.1 12.0 %all-to-all-done.2 = bf16[5,8,8,768]{3,1,0,2:T(8,128)(2,1)S(1)} async-done(((bf16[5,8,8,768]{3,1,0,2:T(8,128)(2,1)}), bf16[5,8,8,768]{3,1,0,2:T(8,128)(2,1)S(1)}, u32[]{:S(2)}, u32[]{:S(2)}) %all-to-all-start.2) | async-done | bytes 491552 | tf_op jit(solution)/shard_map/all_to_all | solution.py:123
  82.1 5.5 %all-to-all-start = ((bf16[5,32,2,768]{3,2,0,1:T(2,128)(2,1)}), bf16[5,32,2,768]{3,2,0,1:T(2,128)(2,1)S(1)}, u32[]{:S(2)}, u32[]{:S(2)}) async-start(bf16[5,32,2,768]{3,2,0,1:T(2,128)(2,1)} %copy.146), calls=%async_computation | async-start | bytes 983040 | tf_op jit(solution)/shard_map/all_to_all | solution.py:126
  87.6 1.3 copy.158
  88.9 11.4 %all-to-all-done = bf16[5,32,2,768]{3,2,0,1:T(2,128)(2,1)S(1)} async-done(((bf16[5,32,2,768]{3,2,0,1:T(2,128)(2,1)}), bf16[5,32,2,768]{3,2,0,1:T(2,128)(2,1)S(1)}, u32[]{:S(2)}, u32[]{:S(2)}) %all-to-all-start) | async-done | bytes 491552 | tf_op jit(solution)/shard_map/all_to_all | solution.py:126
  100.3 3.7 %all-to-all-start.3 = ((bf16[5,32,2,768]{3,2,0,1:T(2,128)(2,1)}), bf16[5,32,2,768]{3,2,0,1:T(2,128)(2,1)S(1)}, u32[]{:S(2)}, u32[]{:S(2)}) async-start(bf16[5,32,2,768]{3,2,0,1:T(2,128)(2,1)} %copy.158), calls=%async_computation.3 | async-start | bytes 983040 | tf_op jit(solution)/shard_map/all_to_all | solution.py:125
  104.6 2.8 %fusion.43 = bf16[40,8,6,128]{3,1,2,0:T(8,128)(2,1)} fusion(bf16[40,8,768]{2,1,0:T(8,128)(2,1)S(1)} %reshape.134, bf16[768,768]{1,0:T(8,128)(2,1)} %all-gather.11.cloned.1.call-done), kind=kOutput, calls=%fused_computation.49 | convolution fusion | flops 377733120 | bytes 2162688 | tf_op jit(solution)/shard_map/dot_general | solution.py:65
  107.4 9.7 %all-to-all-done.3 = bf16[5,32,2,768]{3,2,0,1:T(2,128)(2,1)S(1)} async-done(((bf16[5,32,2,768]{3,2,0,1:T(2,128)(2,1)}), bf16[5,32,2,768]{3,2,0,1:T(2,128)(2,1)S(1)}, u32[]{:S(2)}, u32[]{:S(2)}) %all-to-all-start.3) | async-done | bytes 491552 | tf_op jit(solution)/shard_map/all_to_all | solution.py:125
  117.9 0.8 copy.164
  119.0 0.7 reshape.159
  119.7 3.4 %convolution_convert_fusion = bf16[40,8,2304]{2,1,0:T(8,128)(2,1)S(1)} fusion(bf16[768,2304]{1,0:T(8,128)(2,1)} %all-gather.9.cloned.1.call-done, f32[40,8,768]{2,1,0:T(8,128)S(1)} %reshape.159, f32[768]{0:T(1024)S(1)} %copy-done.7, f32[40,8]{1,0:T(8,128)S(1)} %copy.163), kind=kOutput, calls=%fused_computation.4 | convolution fusion | flops 1133936640 | bytes 6000896 | tf_op jit(solution)/shard_map/dot_general | solution.py:26
  123.1 0.9 slice_bitcast_fusion
  124.2 0.4 fusion.60
  124.6 2.6 %fusion.106 = (f32[8,6,40]{2,1,0:T(8,128)S(1)}, f32[8,6,40,40]{2,3,1,0:T(8,128)}) fusion(bf16[40,8,6,128]{3,1,2,0:T(8,128)(2,1)S(1)} %get-tuple-element.7, bf16[40,8,6,128]{3,1,2,0:T(8,128)(2,1)} %get-tuple-element.6), kind=kOutput, calls=%fused_computation.127 | convolution fusion | flops 19891240 | bytes 1297920 | tf_op jit(solution)/shard_map/sub | solution.py:41
  127.2 2.6 %fusion.48 = bf16[40,8,6,128]{3,0,2,1:T(8,128)(2,1)} fusion(bf16[40,8,6,128]{3,1,2,0:T(8,128)(2,1)} %fusion.43, f32[8,6,40,40]{2,3,1,0:T(8,128)} %get-tuple-element.11, f32[8,6,40]{2,1,0:T(8,128)S(1)} %get-tuple-element.10), kind=kOutput, calls=%fused_computation.54 | convolution fusion | flops 20060160 | bytes 1297920 | tf_op jit(solution)/shard_map/bhlm,lbhe->mbhe/dot_general | solution.py:70
  129.8 3.0 %fusion.47 = bf16[40,8,6,128]{3,0,2,1:T(8,128)(2,1)} fusion(f32[8,6,40,40]{2,3,1,0:T(8,128)S(1)} %fusion.60, bf16[40,8,6,128]{3,1,2,0:T(8,128)(2,1)} %get-tuple-element.6, f32[8,6,40,40]{2,3,1,0:T(8,128)} %get-tuple-element.11, f32[8,6,40]{2,1,0:T(8,128)S(1)} %get-tuple-element.10), kind=kOutput, calls=%fused_computation.53 | convolution fusion | flops 20446120 | bytes 1605120 | tf_op jit(solution)/shard_map/bhlm,lbhe->mbhe/dot_general | solution.py:78
  132.8 2.9 %fusion.46 = bf16[40,8,6,128]{3,0,2,1:T(8,128)(2,1)} fusion(f32[8,6,40,40]{2,3,1,0:T(8,128)S(1)} %fusion.60, bf16[40,8,6,128]{3,1,2,0:T(8,128)(2,1)S(1)} %get-tuple-element.7, f32[8,6,40,40]{2,3,1,0:T(8,128)} %get-tuple-element.11, f32[8,6,40]{2,1,0:T(8,128)S(1)} %get-tuple-element.10), kind=kOutput, calls=%fused_computation.52 | convolution fusion | flops 20446120 | bytes 1605120 | tf_op jit(solution)/shard_map/bhlm,mbhe->lbhe/dot_general | solution.py:75
  135.7 1.2 copy.231
  136.8 1.4 copy_bitcast_fusion.3
  138.2 3.5 %multiply_reduce_fusion.2 = (f32[40,8]{1,0:T(8,128)S(1)}, f32[40,8,768]{2,1,0:T(8,128)S(1)}) fusion(f32[40,8,768]{2,1,0:T(8,128)S(1)} %reshape.159, f32[768]{0:T(1024)S(1)} %copy-done.7, bf16[768,2304]{1,0:T(8,128)(2,1)} %all-gather.9.cloned.1.call-done, bf16[40,8,768]{2,1,0:T(8,128)(2,1)S(1)} %get-tuple-element.16, ...), kind=kOutput, calls=%fused_computation.68 | convolution fusion | flops 1137622784 | bytes 6983936 | tf_op jit(solution)/shard_map/dot_general | solution.py:84
  142.2 17.2 %all_to_all.103 = bf16[40,4,2,768]{3,2,1,0:T(2,128)(2,1)S(1)} all-to-all(bf16[40,4,2,768]{3,2,1,0:T(2,128)(2,1)S(1)} %reshape.147), channel_id=1, replica_groups=mesh['tr'=4,'gz'=8] {'gz'}, dimensions={0} | all-to-all | bytes 983040 | tf_op jit(solution)/shard_map/all_to_all | solution.py:129
  160.2 10.9 %all_to_all.104 = bf16[5,32,2,768]{3,2,0,1:T(2,128)(2,1)S(1)} all-to-all(bf16[5,32,2,768]{3,2,0,1:T(2,128)(2,1)S(1)} %copy.178), channel_id=1, replica_groups=mesh['tr'=4,'gz'=8] {'tr'}, dimensions={1} | all-to-all | bytes 983040 | tf_op jit(solution)/shard_map/all_to_all | solution.py:130
  171.1 0.5 copy.180
  171.8 0.5 copy-done.6
  172.3 0.6 fusion.44
  172.9 0.6 copy-done.9
  173.5 1.2 fusion.51
  174.7 1.5 fusion.79
  176.3 2.7 %fusion.49 = bf16[40,8,768]{2,1,0:T(8,128)(2,1)} fusion(f32[40,6,8,8]{2,3,1,0:T(8,128)S(1)} %fusion.79, bf16[40,8,2304]{2,1,0:T(8,128)(2,1)} %copy-done.5, f32[40,6,8,8]{2,3,1,0:T(8,128)S(1)} %copy-done.10, f32[40,6,8]{2,1,0:T(8,128)} %copy-done.11), kind=kOutput, calls=%fused_computation.55 | convolution fusion | flops 4287367 | bytes 5242880 | tf_op jit(solution)/shard_map/bhlm,bmhe->blhe/dot_general | solution.py:75
  179.0 2.6 %fusion.50 = bf16[40,8,768]{2,1,0:T(8,128)(2,1)} fusion(f32[40,6,8,8]{2,3,1,0:T(8,128)S(1)} %fusion.79, bf16[40,8,2304]{2,1,0:T(8,128)(2,1)} %copy-done.5, f32[40,6,8,8]{2,3,1,0:T(8,128)S(1)} %copy-done.10, f32[40,6,8]{2,1,0:T(8,128)} %copy-done.11), kind=kOutput, calls=%fused_computation.56 | convolution fusion | flops 4287367 | bytes 5242880 | tf_op jit(solution)/shard_map/bhlm,blhe->bmhe/dot_general | solution.py:78
  181.6 3.9 %multiply_reduce_fusion.1 = (f32[40,8]{1,0:T(8,128)S(1)}, f32[40,8,768]{2,1,0:T(8,128)S(1)}) fusion(f32[40,8,768]{2,1,0:T(8,128)S(1)} %reshape.154, f32[768]{0:T(1024)S(1)} %copy-done.8, bf16[768,2304]{1,0:T(8,128)(2,1)} %all-gather.5.cloned.1.call-done, bf16[40,8,768]{2,1,0:T(8,128)(2,1)} %fusion.51, bf16[40,8,768]{2,1,0:T(8,128)(2,1)} %fusion.50, ...), kind=kOutput, calls=%fused_computation.66 | convolution fusion | flops 1137622784 | bytes 6983936 | tf_op jit(solution)/shard_map/dot_general | solution.py:84
  185.9 10.9 %all_to_all.105 = bf16[5,8,8,768]{3,1,0,2:T(8,128)(2,1)S(1)} all-to-all(bf16[5,8,8,768]{3,1,0,2:T(8,128)(2,1)S(1)} %copy.182), channel_id=1, replica_groups=mesh['tr'=4,'gz'=8] {'tr'}, dimensions={2} | all-to-all | bytes 983040 | tf_op jit(solution)/shard_map/all_to_all | solution.py:132
  196.8 1.2 copy.183
  (57 shorter events, 4.6 us)
Async XLA Ops:
  6.5 2.8 %copy-start.2 = (bf16[5,32,2,768]{3,2,1,0:T(2,128)(2,1)S(1)}, bf16[5,32,2,768]{3,2,1,0:T(2,128)(2,1)}, u32[]{:S(2)}) copy-start(bf16[5,32,2,768]{3,2,1,0:T(2,128)(2,1)} %param.8) | copy-start | bytes 1474564
  6.5 36.2 %all-gather.5.cloned.1.call-start = ((), (), s32[]{:S(2)}) async-start(), calls=%async_computation.7 | async-start | bytes 4423680 | tf_op jit(solution)/shard_map/all_gather | solution.py:114
  7.3 54.8 %all-gather.7.cloned.1.call-start = ((), (), s32[]{:S(2)}) async-start(), calls=%async_computation.8 | async-start | bytes 1474560 | tf_op jit(solution)/shard_map/all_gather | solution.py:115
  8.0 96.6 %all-gather.11.cloned.1.call-start = ((), (), s32[]{:S(2)}) async-start(), calls=%async_computation.10 | async-start | bytes 1474560 | tf_op jit(solution)/shard_map/all_gather | solution.py:119
  8.7 111.0 %all-gather.9.cloned.1.call-start = ((), (), s32[]{:S(2)}) async-start(), calls=%async_computation.9 | async-start | bytes 4423680 | tf_op jit(solution)/shard_map/all_gather | solution.py:118
  23.6 19.1 %copy-start.8 = (f32[768]{0:T(1024)S(1)}, f32[768]{0:T(1024)}, u32[]{:S(2)}) copy-start(f32[768]{0:T(1024)} %param.10) | copy-start | bytes 9220
  46.1 16.0 %copy-start.5 = (bf16[40,8,2304]{2,1,0:T(8,128)(2,1)}, bf16[40,8,2304]{2,1,0:T(8,128)(2,1)S(1)}, u32[]{:S(2)}) copy-start(bf16[40,8,2304]{2,1,0:T(8,128)(2,1)S(1)} %convolution_convert_fusion.1) | copy-start | bytes 4423684
  47.9 16.7 %copy-start.11 = (f32[40,6,8]{2,1,0:T(8,128)}, f32[40,6,8]{2,1,0:T(8,128)S(1)}, u32[]{:S(2)}) copy-start(f32[40,6,8]{2,1,0:T(8,128)S(1)} %get-tuple-element.8) | copy-start | bytes 23044
  64.6 4.4 %copy-start.3 = (bf16[5,32,2,768]{3,2,1,0:T(2,128)(2,1)S(1)}, bf16[5,32,2,768]{3,2,1,0:T(2,128)(2,1)}, u32[]{:S(2)}) copy-start(bf16[5,32,2,768]{3,2,1,0:T(2,128)(2,1)} %param.9) | copy-start | bytes 1474564
  65.5 16.6 %all-to-all-start.2 = ((bf16[5,8,8,768]{3,1,0,2:T(8,128)(2,1)}), bf16[5,8,8,768]{3,1,0,2:T(8,128)(2,1)S(1)}, u32[]{:S(2)}, u32[]{:S(2)}) async-start(bf16[5,8,8,768]{3,1,0,2:T(8,128)(2,1)} %copy.155), calls=%async_computation.2 | async-start | bytes 983040 | tf_op jit(solution)/shard_map/all_to_all | solution.py:123
  82.1 18.3 %all-to-all-start = ((bf16[5,32,2,768]{3,2,0,1:T(2,128)(2,1)}), bf16[5,32,2,768]{3,2,0,1:T(2,128)(2,1)S(1)}, u32[]{:S(2)}, u32[]{:S(2)}) async-start(bf16[5,32,2,768]{3,2,0,1:T(2,128)(2,1)} %copy.146), calls=%async_computation | async-start | bytes 983040 | tf_op jit(solution)/shard_map/all_to_all | solution.py:126
  100.3 16.8 %all-to-all-start.3 = ((bf16[5,32,2,768]{3,2,0,1:T(2,128)(2,1)}), bf16[5,32,2,768]{3,2,0,1:T(2,128)(2,1)S(1)}, u32[]{:S(2)}, u32[]{:S(2)}) async-start(bf16[5,32,2,768]{3,2,0,1:T(2,128)(2,1)} %copy.158), calls=%async_computation.3 | async-start | bytes 983040 | tf_op jit(solution)/shard_map/all_to_all | solution.py:125
  104.5 13.1 %copy-start = (bf16[40,8,768]{2,1,0:T(8,128)(2,1)}, bf16[40,8,768]{2,1,0:T(8,128)(2,1)S(1)}, u32[]{:S(2)}) copy-start(bf16[40,8,768]{2,1,0:T(8,128)(2,1)S(1)} %reshape.134) | copy-start | bytes 1474564
  119.0 0.7 copy-start.7
  123.1 1.1 copy-start.4
  138.2 3.5 %copy-start.1 = (bf16[40,8,768]{2,1,0:T(8,128)(2,1)S(1)}, bf16[40,8,768]{2,1,0:T(8,128)(2,1)}, u32[]{:S(2)}) copy-start(bf16[40,8,768]{2,1,0:T(8,128)(2,1)} %copy-done) | copy-start | bytes 1474564
  171.1 1.3 copy-start.6
  171.6 1.3 copy-start.12
  172.3 1.2 copy-start.9
  174.7 1.5 copy-start.10
Sparse Core Ops, SparseCore 0:
  8.9 33.7 all-gather.4
  44.3 17.7 all-gather.6
  63.7 21.5 all-gather.10
  86.6 30.7 all-gather.8
where the time goes:
time: 205 us; the launch traced here: 204 us
  waiting for transfers between devices  68.1 us (33%)
  blocking collectives  52 us (25%)
  matrix products  41.2 us (20%)
  local copies, waits for them, and re-layouts  15 us (7%)
  between operations  13.5 us (7%)
  starting transfers between devices  12.8 us (6%)
    all_gather x1, waiting for transfers between devices, per_device(): lax.all_gather(wqkv_x, 'tr', axis=0, tiled=True)  18 us
    all_to_all x1, blocking collectives, per_device(): lax.all_to_all(grad_columns, 'gz', split_axis=0, concat_axis=1, tiled=True)  17.2 us
    all_gather x1, waiting for transfers between devices, per_device(): lax.all_gather(wo_x, 'tr', axis=0, tiled=True)  14.2 us
    all_to_all x1, blocking collectives, per_device(): lax.all_to_all(tokens, 'tr', split_axis=1, concat_axis=2, tiled=True)  13 us
    all_to_all x1, waiting for transfers between devices, per_device(): lax.all_to_all(mid_lines, 'tr', split_axis=2, concat_axis=1, tiled=True)  12 us
    all_to_all x1, waiting for transfers between devices, per_device(): lax.all_to_all(cotangent, 'gz', split_axis=1, concat_axis=0, tiled=True)  11.4 us
    all_to_all x1, blocking collectives, per_device(): lax.all_to_all(grad_home, 'tr', split_axis=1, concat_axis=2, tiled=True)  10.9 us
    all_to_all x1, blocking collectives, per_device(): lax.all_to_all(result_lines, 'tr', split_axis=2, concat_axis=1, tiled=True)  10.9 us
  transfers between devices with their start and end apart: 7, of which 5 were waited for; matrix products, arithmetic and copies ran while one was open for 9% of the time, Pallas kernels for 0%

commit v1 on v0

--- a/solution.py
+++ b/solution.py
@@ -102,13 +102,6 @@
     return backward(flat, flat_up, gain_vec, w_in, w_out, "blhe").reshape(lines.shape)
 
 
-def column_backward(columns, upstream, gain_vec, w_in, w_out):
-    feature_count = columns.shape[3]
-    flat = columns.reshape(columns.shape[0], -1, feature_count)
-    flat_up = upstream.reshape(flat.shape)
-    return backward(flat, flat_up, gain_vec, w_in, w_out, "lbhe").reshape(columns.shape)
-
-
 def per_device(tokens, cotangent, gain_x, wqkv_x, wo_x, gain_z, wqkv_z, wo_z):
     full_in_x, full_out_x = (
         lax.all_gather(wqkv_x, "tr", axis=0, tiled=True),
@@ -118,17 +111,23 @@
         lax.all_gather(wqkv_z, "tr", axis=0, tiled=True),
         lax.all_gather(wo_z, "tr", axis=0, tiled=True),
     )
+    width = tokens.shape[-1]
     lines = lax.all_to_all(tokens, "tr", split_axis=1, concat_axis=2, tiled=True)
+    cot_lines = lax.all_to_all(cotangent, "tr", split_axis=1, concat_axis=2, tiled=True)
+    cells = lines.shape[1] * lines.shape[2]
+    flat = (lines.shape[0], cells, width)
+    cot_columns = lax.all_to_all(
+        cot_lines.reshape(flat), "gz", split_axis=1, concat_axis=0, tiled=True
+    )
     mid_lines = line_forward(lines, gain_x, full_in_x, full_out_x)
-    mid_home = lax.all_to_all(mid_lines, "tr", split_axis=2, concat_axis=1, tiled=True)
-    mid_columns, cot_columns = (
-        lax.all_to_all(mid_home, "gz", split_axis=1, concat_axis=0, tiled=True),
-        lax.all_to_all(cotangent, "gz", split_axis=1, concat_axis=0, tiled=True),
+    mid_columns = lax.all_to_all(
+        mid_lines.reshape(flat), "gz", split_axis=1, concat_axis=0, tiled=True
     )
-    grad_columns = column_backward(mid_columns, cot_columns, gain_z, full_in_z, full_out_z)
-    grad_home = lax.all_to_all(grad_columns, "gz", split_axis=0, concat_axis=1, tiled=True)
-    grad_lines = lax.all_to_all(grad_home, "tr", split_axis=1, concat_axis=2, tiled=True)
-    result_lines = line_backward(lines, grad_lines, gain_x, full_in_x, full_out_x)
+    grad_columns = backward(
+        mid_columns, cot_columns, gain_z, full_in_z, full_out_z, "lbhe"
+    )
+    grad_lines = lax.all_to_all(grad_columns, "gz", split_axis=0, concat_axis=1, tiled=True)
+    result_lines = line_backward(lines, grad_lines.reshape(lines.shape), gain_x, full_in_x, full_out_x)
     return lax.all_to_all(result_lines, "tr", split_axis=2, concat_axis=1, tiled=True)
 
 

time: 205 us -> 195 us (0.951)
  blocking collectives: 52 us -> 30.5 us
  starting transfers between devices: 12.8 us -> 20.6 us
  waiting for transfers between devices: 68.1 us -> 75.3 us
  local copies, waits for them, and re-layouts: 15 us -> 11.4 us
    all_to_all x2 -> x0, blocking collectives: 23.9 us -> none  [the longest x1 13 us: per_device(): lax.all_to_all(tokens, 'tr', split_axis=1, concat_axis=2, tiled=True)]
    all_gather x1, waiting for transfers between devices: 0.02 us -> 20.7 us  [per_device(): lax.all_gather(wqkv_z, 'tr', axis=0, tiled=True)]
    all_gather x1, waiting for transfers between devices: 18 us -> 0.02 us  [per_device(): lax.all_gather(wqkv_x, 'tr', axis=0, tiled=True)]
    all_gather x1, waiting for transfers between devices: 0.02 us -> 9.53 us  [per_device(): lax.all_gather(wo_z, 'tr', axis=0, tiled=True)]
    all_to_all x3 -> x4, starting transfers between devices: 12.7 us -> 20.5 us  [the longest x1 7.34 us: per_device(): lax.all_to_all(cot_lines.reshape(flat), 'gz', split_axis=1, concat_axis=0...]
    all_to_all x3 -> x4, waiting for transfers between devices: 33.1 us -> 30.5 us  [the longest x1 13.1 us: per_device(): lax.all_to_all(cotangent, 'tr', split_axis=1, concat_axis=2, tiled=True)]
    all_to_all x1, blocking collectives: 17.2 us -> 19.6 us  [per_device(): lax.all_to_all(grad_columns, 'gz', split_axis=0, concat_axis=1, tiled=True)]
    all_gather x1, waiting for transfers between devices: 14.2 us -> 11.9 us  [per_device(): lax.all_gather(wo_x, 'tr', axis=0, tiled=True)]
  transfers between devices with their start and end apart: 7 -> 8, of which waited for: 5 -> 6; matrix products, arithmetic and copies ran while one was open for 9% -> 9% of each run, Pallas kernels for 0% -> 0%
where the time goes in v1:
time: 195 us; the launch traced here: 194 us
  waiting for transfers between devices  75.3 us (39%)
  matrix products  41.2 us (21%)
  blocking collectives  30.5 us (16%)
  starting transfers between devices  20.6 us (11%)
  between operations  13.4 us (7%)
  local copies, waits for them, and re-layouts  11.4 us (6%)
    all_gather x1, waiting for transfers between devices, per_device(): lax.all_gather(wqkv_z, 'tr', axis=0, tiled=True)  20.7 us
    all_to_all x1, blocking collectives, per_device(): lax.all_to_all(grad_columns, 'gz', split_axis=0, concat_axis=1, tiled=True)  19.6 us
    all_to_all x1, waiting for transfers between devices, per_device(): lax.all_to_all(cotangent, 'tr', split_axis=1, concat_axis=2, tiled=True)  13.1 us
    all_gather x1, waiting for transfers between devices, per_device(): lax.all_gather(wo_x, 'tr', axis=0, tiled=True)  11.9 us
    all_to_all x1, blocking collectives, per_device(): lax.all_to_all(result_lines, 'tr', split_axis=2, concat_axis=1, tiled=True)  10.9 us
    all_gather x1, waiting for transfers between devices, per_device(): lax.all_gather(wo_z, 'tr', axis=0, tiled=True)  9.53 us
    all_to_all x1, waiting for transfers between devices, per_device(): lax.all_to_all(tokens, 'tr', split_axis=1, concat_axis=2, tiled=True)  9.19 us
    all_to_all x1, waiting for transfers between devices, per_device(): lax.all_to_all(mid_lines.reshape(flat), 'gz', split_axis=1, concat_axis=0...  8.26 us
  transfers between devices with their start and end apart: 8, of which 6 were waited for; matrix products, arithmetic and copies ran while one was open for 9% of the time, Pallas kernels for 0%

profile of v1, /device:TPU:0, one launch (start us, length us, event | category | flops | bytes accessed | tf_op | source)
XLA Modules:
  0.0 194.4 jit_solution(14103475853062895245)
XLA Ops:
  6.5 0.7 all-gather.5.cloned.1.call-update
  7.3 0.7 all-gather.7.cloned.1.call-update
  8.1 0.7 all-gather.11.cloned.1.call-update
  8.8 0.5 all-gather.9.cloned.1.call-update
  9.3 1.1 copy.114
  10.5 4.2 %all-to-all-start.2 = ((bf16[5,32,2,768]{3,2,0,1:T(2,128)(2,1)}), bf16[5,32,2,768]{3,2,0,1:T(2,128)(2,1)S(1)}, u32[]{:S(2)}, u32[]{:S(2)}) async-start(bf16[5,32,2,768]{3,2,0,1:T(2,128)(2,1)} %copy.114), calls=%async_computation.2 | async-start | bytes 983040 | tf_op jit(solution)/shard_map/all_to_all | solution.py:115
  14.7 1.1 copy.109
  15.8 9.2 %all-to-all-done.2 = bf16[5,32,2,768]{3,2,0,1:T(2,128)(2,1)S(1)} async-done(((bf16[5,32,2,768]{3,2,0,1:T(2,128)(2,1)}), bf16[5,32,2,768]{3,2,0,1:T(2,128)(2,1)S(1)}, u32[]{:S(2)}, u32[]{:S(2)}) %all-to-all-start.2) | async-done | bytes 491552 | tf_op jit(solution)/shard_map/all_to_all | solution.py:115
  25.0 3.5 %all-to-all-start = ((bf16[5,32,2,768]{3,2,0,1:T(2,128)(2,1)}), bf16[5,32,2,768]{3,2,0,1:T(2,128)(2,1)S(1)}, u32[]{:S(2)}, u32[]{:S(2)}) async-start(bf16[5,32,2,768]{3,2,0,1:T(2,128)(2,1)} %copy.109), calls=%async_computation | async-start | bytes 983040 | tf_op jit(solution)/shard_map/all_to_all | solution.py:116
  28.4 0.6 multiply_reduce_fusion.4
  29.4 13.1 %all-to-all-done = bf16[5,32,2,768]{3,2,0,1:T(2,128)(2,1)S(1)} async-done(((bf16[5,32,2,768]{3,2,0,1:T(2,128)(2,1)}), bf16[5,32,2,768]{3,2,0,1:T(2,128)(2,1)S(1)}, u32[]{:S(2)}, u32[]{:S(2)}) %all-to-all-start) | async-done | bytes 491552 | tf_op jit(solution)/shard_map/all_to_all | solution.py:116
  42.5 1.0 copy.144
  43.5 7.3 %all-to-all-start.1 = ((bf16[5,64,768]{2,0,1:T(8,128)(2,1)}), bf16[5,64,768]{2,0,1:T(8,128)(2,1)S(1)}, u32[]{:S(2)}, u32[]{:S(2)}) async-start(bf16[5,64,768]{2,0,1:T(8,128)(2,1)} %bitcast.2), calls=%async_computation.1 | async-start | bytes 1572864 | tf_op jit(solution)/shard_map/all_to_all | solution.py:119
  50.8 0.4 copy_bitcast_fusion
  51.2 0.7 reshape.140
  51.9 3.4 %convolution_convert_fusion.1 = bf16[40,8,2304]{2,1,0:T(8,128)(2,1)S(1)} fusion(bf16[768,2304]{1,0:T(8,128)(2,1)} %all-gather.5.cloned.1.call-done, f32[40,8,768]{2,1,0:T(8,128)S(1)} %reshape.140, f32[768]{0:T(1024)S(1)} %copy-done.8, f32[40,8]{1,0:T(8,128)S(1)} %copy.119), kind=kOutput, calls=%fused_computation.5 | convolution fusion | flops 1133936640 | bytes 6000896 | tf_op jit(solution)/shard_map/dot_general | solution.py:26
  55.3 1.8 fusion.105
  57.1 11.9 %all-gather.7.cloned.1.call-done = bf16[768,768]{1,0:T(8,128)(2,1)} async-done(((bf16[192,768]{1,0:T(8,128)(2,1)}), bf16[768,768]{1,0:T(8,128)(2,1)}) %all-gather.7.cloned.1.call-update) | async-done | bytes 1179664 | tf_op jit(solution)/shard_map/all_gather | solution.py:108
  69.0 2.6 %fusion.40 = bf16[40,8,768]{2,1,0:T(8,128)(2,1)S(1)} fusion(f32[40,8,768]{2,1,0:T(8,128)S(1)} %reshape.140, bf16[768,768]{1,0:T(8,128)(2,1)} %all-gather.7.cloned.1.call-done, bf16[40,8,2304]{2,1,0:T(8,128)(2,1)} %copy-done.5, f32[40,6,8,8]{2,3,1,0:T(8,128)} %get-tuple-element.9, f32[40,6,8]{2,1,0:T(8,128)S(1)} %get-tuple-element.8), kind=kOutput, calls=%fused_computation.38 | convolution fusion | flops 382187520 | bytes 4136448 | tf_op jit(solution)/shard_map/dot_general | solution.py:55
  71.7 1.2 copy.121
  72.9 5.5 %all-to-all-start.3 = ((bf16[5,64,768]{2,0,1:T(8,128)(2,1)}), bf16[5,64,768]{2,0,1:T(8,128)(2,1)S(1)}, u32[]{:S(2)}, u32[]{:S(2)}) async-start(bf16[5,64,768]{2,0,1:T(8,128)(2,1)} %copy.121), calls=%async_computation.3 | async-start | bytes 1572864 | tf_op jit(solution)/shard_map/all_to_all | solution.py:123
  78.5 9.5 %all-gather.11.cloned.1.call-done = bf16[768,768]{1,0:T(8,128)(2,1)} async-done(((bf16[192,768]{1,0:T(8,128)(2,1)}), bf16[768,768]{1,0:T(8,128)(2,1)}) %all-gather.11.cloned.1.call-update) | async-done | bytes 1179664 | tf_op jit(solution)/shard_map/all_gather | solution.py:112
  88.1 2.6 %fusion.43 = bf16[40,8,6,128]{3,1,2,0:T(8,128)(2,1)} fusion(bf16[40,8,768]{2,1,0:T(8,128)(2,1)S(1)} %bitcast.138, bf16[768,768]{1,0:T(8,128)(2,1)} %all-gather.11.cloned.1.call-done), kind=kOutput, calls=%fused_computation.50 | convolution fusion | flops 377733120 | bytes 2162688 | tf_op jit(solution)/shard_map/dot_general | solution.py:65
  90.7 8.3 %all-to-all-done.3 = bf16[5,64,768]{2,0,1:T(8,128)(2,1)S(1)} async-done(((bf16[5,64,768]{2,0,1:T(8,128)(2,1)}), bf16[5,64,768]{2,0,1:T(8,128)(2,1)S(1)}, u32[]{:S(2)}, u32[]{:S(2)}) %all-to-all-start.3) | async-done | bytes 491552 | tf_op jit(solution)/shard_map/all_to_all | solution.py:123
  99.0 0.3 multiply_reduce_fusion
  99.6 20.7 %all-gather.9.cloned.1.call-done = bf16[768,2304]{1,0:T(8,128)(2,1)} async-done(((bf16[192,2304]{1,0:T(8,128)(2,1)}), bf16[768,2304]{1,0:T(8,128)(2,1)}) %all-gather.9.cloned.1.call-update) | async-done | bytes 3538960 | tf_op jit(solution)/shard_map/all_gather | solution.py:111
  120.3 3.3 %convolution_convert_fusion = bf16[40,8,2304]{2,1,0:T(8,128)(2,1)S(1)} fusion(bf16[768,2304]{1,0:T(8,128)(2,1)} %all-gather.9.cloned.1.call-done, f32[40,8,768]{2,1,0:T(8,128)S(1)} %bitcast.135, f32[768]{0:T(1024)S(1)} %copy-done.7, f32[40,8]{1,0:T(8,128)S(1)} %reshape.158), kind=kOutput, calls=%fused_computation.4 | convolution fusion | flops 1133936640 | bytes 6000896 | tf_op jit(solution)/shard_map/dot_general | solution.py:26
  123.7 0.9 slice_bitcast_fusion
  124.8 0.4 fusion.60
  125.2 2.6 %fusion.106 = (f32[8,6,40]{2,1,0:T(8,128)S(1)}, f32[8,6,40,40]{2,3,1,0:T(8,128)}) fusion(bf16[40,8,6,128]{3,1,2,0:T(8,128)(2,1)S(1)} %get-tuple-element.7, bf16[40,8,6,128]{3,1,2,0:T(8,128)(2,1)} %get-tuple-element.6), kind=kOutput, calls=%fused_computation.123 | convolution fusion | flops 19891240 | bytes 1297920 | tf_op jit(solution)/shard_map/sub | solution.py:41
  127.8 2.6 %fusion.48 = bf16[40,8,6,128]{3,0,2,1:T(8,128)(2,1)} fusion(bf16[40,8,6,128]{3,1,2,0:T(8,128)(2,1)} %fusion.43, f32[8,6,40,40]{2,3,1,0:T(8,128)} %get-tuple-element.11, f32[8,6,40]{2,1,0:T(8,128)S(1)} %get-tuple-element.10), kind=kOutput, calls=%fused_computation.55 | convolution fusion | flops 20060160 | bytes 1297920 | tf_op jit(solution)/shard_map/bhlm,lbhe->mbhe/dot_general | solution.py:70
  130.3 3.0 %fusion.47 = bf16[40,8,6,128]{3,0,2,1:T(8,128)(2,1)} fusion(f32[8,6,40,40]{2,3,1,0:T(8,128)S(1)} %fusion.60, bf16[40,8,6,128]{3,1,2,0:T(8,128)(2,1)} %get-tuple-element.6, f32[8,6,40,40]{2,3,1,0:T(8,128)} %get-tuple-element.11, f32[8,6,40]{2,1,0:T(8,128)S(1)} %get-tuple-element.10), kind=kOutput, calls=%fused_computation.54 | convolution fusion | flops 20446120 | bytes 1605120 | tf_op jit(solution)/shard_map/bhlm,lbhe->mbhe/dot_general | solution.py:78
  133.3 2.9 %fusion.46 = bf16[40,8,6,128]{3,0,2,1:T(8,128)(2,1)} fusion(f32[8,6,40,40]{2,3,1,0:T(8,128)S(1)} %fusion.60, bf16[40,8,6,128]{3,1,2,0:T(8,128)(2,1)S(1)} %get-tuple-element.7, f32[8,6,40,40]{2,3,1,0:T(8,128)} %get-tuple-element.11, f32[8,6,40]{2,1,0:T(8,128)S(1)} %get-tuple-element.10), kind=kOutput, calls=%fused_computation.53 | convolution fusion | flops 20446120 | bytes 1605120 | tf_op jit(solution)/shard_map/bhlm,mbhe->lbhe/dot_general | solution.py:75
  136.3 1.2 copy.183
  137.4 1.4 copy_bitcast_fusion.1
  138.8 3.5 %multiply_reduce_fusion.3 = (f32[40,8]{1,0:T(8,128)S(1)}, f32[40,8,768]{2,1,0:T(8,128)S(1)}) fusion(f32[40,8,768]{2,1,0:T(8,128)S(1)} %bitcast.136, f32[768]{0:T(1024)S(1)} %copy-done.7, bf16[768,2304]{1,0:T(8,128)(2,1)} %all-gather.9.cloned.1.call-done, bf16[40,8,768]{2,1,0:T(8,128)(2,1)S(1)} %get-tuple-element.16, ...), kind=kOutput, calls=%fused_computation.69 | convolution fusion | flops 1137622784 | bytes 6983936 | tf_op jit(solution)/shard_map/dot_general | solution.py:84
  142.3 0.3 add_convert_fusion.1
  142.6 19.6 %all_to_all.84 = bf16[40,8,768]{2,1,0:T(8,128)(2,1)S(1)} all-to-all(bf16[40,8,768]{2,1,0:T(8,128)(2,1)S(1)} %add_convert_fusion.1), channel_id=1, replica_groups=mesh['tr'=4,'gz'=8] {'gz'}, dimensions={0} | all-to-all | bytes 983040 | tf_op jit(solution)/shard_map/all_to_all | solution.py:129
  162.3 0.6 fusion.44
  162.9 0.6 copy-done.9
  163.5 1.2 fusion.51
  164.7 1.5 fusion.79
  166.2 2.7 %fusion.49 = bf16[40,8,768]{2,1,0:T(8,128)(2,1)} fusion(f32[40,6,8,8]{2,3,1,0:T(8,128)S(1)} %fusion.79, bf16[40,8,2304]{2,1,0:T(8,128)(2,1)} %copy-done.5, f32[40,6,8,8]{2,3,1,0:T(8,128)S(1)} %copy-done.10, f32[40,6,8]{2,1,0:T(8,128)} %copy-done.11), kind=kOutput, calls=%fused_computation.56 | convolution fusion | flops 4287367 | bytes 5242880 | tf_op jit(solution)/shard_map/bhlm,bmhe->blhe/dot_general | solution.py:75
  168.9 2.6 %fusion.50 = bf16[40,8,768]{2,1,0:T(8,128)(2,1)} fusion(f32[40,6,8,8]{2,3,1,0:T(8,128)S(1)} %fusion.79, bf16[40,8,2304]{2,1,0:T(8,128)(2,1)} %copy-done.5, f32[40,6,8,8]{2,3,1,0:T(8,128)S(1)} %copy-done.10, f32[40,6,8]{2,1,0:T(8,128)} %copy-done.11), kind=kOutput, calls=%fused_computation.57 | convolution fusion | flops 4287367 | bytes 5242880 | tf_op jit(solution)/shard_map/bhlm,blhe->bmhe/dot_general | solution.py:78
  171.5 3.9 %multiply_reduce_fusion.2 = (f32[40,8]{1,0:T(8,128)S(1)}, f32[40,8,768]{2,1,0:T(8,128)S(1)}) fusion(f32[40,8,768]{2,1,0:T(8,128)S(1)} %reshape.140, f32[768]{0:T(1024)S(1)} %copy-done.8, bf16[768,2304]{1,0:T(8,128)(2,1)} %all-gather.5.cloned.1.call-done, bf16[40,8,768]{2,1,0:T(8,128)(2,1)} %fusion.51, bf16[40,8,768]{2,1,0:T(8,128)(2,1)} %fusion.50, ...), kind=kOutput, calls=%fused_computation.67 | convolution fusion | flops 1137622784 | bytes 6983936 | tf_op jit(solution)/shard_map/dot_general | solution.py:84
  175.4 0.3 add_convert_fusion
  175.9 10.9 %all_to_all.85 = bf16[5,8,8,768]{3,1,0,2:T(8,128)(2,1)S(1)} all-to-all(bf16[5,8,8,768]{3,1,0,2:T(8,128)(2,1)S(1)} %copy.139), channel_id=1, replica_groups=mesh['tr'=4,'gz'=8] {'tr'}, dimensions={2} | all-to-all | bytes 983040 | tf_op jit(solution)/shard_map/all_to_all | solution.py:131
  186.7 1.2 copy.140
  (47 shorter events, 1.3 us)
Async XLA Ops:
  6.5 2.8 %copy-start.2 = (bf16[5,32,2,768]{3,2,1,0:T(2,128)(2,1)S(1)}, bf16[5,32,2,768]{3,2,1,0:T(2,128)(2,1)}, u32[]{:S(2)}) copy-start(bf16[5,32,2,768]{3,2,1,0:T(2,128)(2,1)} %param.8) | copy-start | bytes 1474564
  6.5 45.4 %all-gather.5.cloned.1.call-start = ((), (), s32[]{:S(2)}) async-start(), calls=%async_computation.6 | async-start | bytes 4423680 | tf_op jit(solution)/shard_map/all_gather | solution.py:107
  7.3 61.8 %all-gather.7.cloned.1.call-start = ((), (), s32[]{:S(2)}) async-start(), calls=%async_computation.7 | async-start | bytes 1474560 | tf_op jit(solution)/shard_map/all_gather | solution.py:108
  8.0 80.1 %all-gather.11.cloned.1.call-start = ((), (), s32[]{:S(2)}) async-start(), calls=%async_computation.9 | async-start | bytes 1474560 | tf_op jit(solution)/shard_map/all_gather | solution.py:112
  8.7 5.9 %copy-start.3 = (bf16[5,32,2,768]{3,2,1,0:T(2,128)(2,1)S(1)}, bf16[5,32,2,768]{3,2,1,0:T(2,128)(2,1)}, u32[]{:S(2)}) copy-start(bf16[5,32,2,768]{3,2,1,0:T(2,128)(2,1)} %param.9) | copy-start | bytes 1474564
  8.8 111.5 %all-gather.9.cloned.1.call-start = ((), (), s32[]{:S(2)}) async-start(), calls=%async_computation.8 | async-start | bytes 4423680 | tf_op jit(solution)/shard_map/all_gather | solution.py:111
  10.5 14.5 %all-to-all-start.2 = ((bf16[5,32,2,768]{3,2,0,1:T(2,128)(2,1)}), bf16[5,32,2,768]{3,2,0,1:T(2,128)(2,1)S(1)}, u32[]{:S(2)}, u32[]{:S(2)}) async-start(bf16[5,32,2,768]{3,2,0,1:T(2,128)(2,1)} %copy.114), calls=%async_computation.2 | async-start | bytes 983040 | tf_op jit(solution)/shard_map/all_to_all | solution.py:115
  25.0 17.5 %all-to-all-start = ((bf16[5,32,2,768]{3,2,0,1:T(2,128)(2,1)}), bf16[5,32,2,768]{3,2,0,1:T(2,128)(2,1)S(1)}, u32[]{:S(2)}, u32[]{:S(2)}) async-start(bf16[5,32,2,768]{3,2,0,1:T(2,128)(2,1)} %copy.109), calls=%async_computation | async-start | bytes 983040 | tf_op jit(solution)/shard_map/all_to_all | solution.py:116
  43.5 29.4 %all-to-all-start.1 = ((bf16[5,64,768]{2,0,1:T(8,128)(2,1)}), bf16[5,64,768]{2,0,1:T(8,128)(2,1)S(1)}, u32[]{:S(2)}, u32[]{:S(2)}) async-start(bf16[5,64,768]{2,0,1:T(8,128)(2,1)} %bitcast.2), calls=%async_computation.1 | async-start | bytes 1572864 | tf_op jit(solution)/shard_map/all_to_all | solution.py:119
  50.8 1.1 copy-start.8
  55.3 1.8 copy-start.5
  57.1 14.6 %copy-start.11 = (f32[40,6,8]{2,1,0:T(8,128)}, f32[40,6,8]{2,1,0:T(8,128)S(1)}, u32[]{:S(2)}) copy-start(f32[40,6,8]{2,1,0:T(8,128)S(1)} %get-tuple-element.8) | copy-start | bytes 23044
  72.9 26.1 %all-to-all-start.3 = ((bf16[5,64,768]{2,0,1:T(8,128)(2,1)}), bf16[5,64,768]{2,0,1:T(8,128)(2,1)S(1)}, u32[]{:S(2)}, u32[]{:S(2)}) async-start(bf16[5,64,768]{2,0,1:T(8,128)(2,1)} %copy.121), calls=%async_computation.3 | async-start | bytes 1572864 | tf_op jit(solution)/shard_map/all_to_all | solution.py:123
  78.5 20.7 %copy-start = (bf16[8,5,8,768]{3,2,1,0:T(8,128)(2,1)}, bf16[8,5,8,768]{3,2,1,0:T(8,128)(2,1)S(1)}, u32[]{:S(2)}) copy-start(bf16[8,5,8,768]{3,2,1,0:T(8,128)(2,1)S(1)} %copy.113) | copy-start | bytes 1474564
  90.7 29.6 %copy-start.7 = (f32[768]{0:T(1024)S(1)}, f32[768]{0:T(1024)}, u32[]{:S(2)}) copy-start(f32[768]{0:T(1024)} %param.13) | copy-start | bytes 9220
  123.7 1.1 copy-start.4
  138.8 3.5 %copy-start.1 = (bf16[8,5,8,768]{3,2,1,0:T(8,128)(2,1)S(1)}, bf16[8,5,8,768]{3,2,1,0:T(8,128)(2,1)}, u32[]{:S(2)}) copy-start(bf16[8,5,8,768]{3,2,1,0:T(8,128)(2,1)} %copy-done) | copy-start | bytes 1474564
  142.6 19.7 %copy-start.6 = (bf16[768,768]{1,0:T(8,128)(2,1)S(1)}, bf16[768,768]{1,0:T(8,128)(2,1)}, u32[]{:S(2)}) copy-start(bf16[768,768]{1,0:T(8,128)(2,1)} %all-gather.7.cloned.1.call-done) | copy-start | bytes 3538948
  162.3 1.2 copy-start.9
  162.3 1.2 copy-start.12
  164.7 1.5 copy-start.10
Sparse Core Ops, SparseCore 0:
  8.9 40.0 all-gather.4
  50.5 18.4 all-gather.6
  70.6 17.4 all-gather.10
  89.5 30.7 all-gather.8

commit v2 on v1

--- a/solution.py
+++ b/solution.py
@@ -1,8 +1,12 @@
+import functools
 import math
 
 import jax
 import jax.numpy as jnp
+import numpy as np
 from jax import lax
+from jax.experimental import pallas as pl
+from jax.experimental.pallas import tpu as pltpu
 from jax.sharding import PartitionSpec as P
 
 H = 6
@@ -131,9 +135,350 @@
     return lax.all_to_all(result_lines, "tr", split_axis=2, concat_axis=1, tiled=True)
 
 
+F32, BF16 = jnp.float32, jnp.bfloat16
+
+
+def nt(a, b):
+    return lax.dot_general(a, b, (((1,), (1,)), ((), ())), preferred_element_type=F32)
+
+
+def tn(a, b):
+    return lax.dot_general(a, b, (((0,), (0,)), ((), ())), preferred_element_type=F32)
+
+
+def nn(a, b):
+    return jnp.dot(a, b, preferred_element_type=F32)
+
+
+def flat(value):
+    width = value.shape[-1]
+    return value.astype(F32).reshape(-1, width)
+
+
+def project(a, gain, w, qkv):
+    rows, width = a.shape
+    rstd = lax.rsqrt(jnp.mean(a * a, axis=-1, keepdims=True) + 1e-06)
+    normed = (a * rstd * gain).astype(BF16)
+
+    def part(j, _):
+        cols = pl.ds(pl.multiple_of(j * width, width), width)
+        qkv[:, cols] = nn(normed, w[:, cols]).astype(BF16)
+        return 0
+
+    lax.fori_loop(0, 3, part, 0)
+    return rstd
+
+
+def line_mask(block, line):
+    key = lax.broadcasted_iota(jnp.int32, (block, block), 0) // line
+    query = lax.broadcasted_iota(jnp.int32, (block, block), 1) // line
+    return key == query
+
+
+def softmax_of(q, k, mask, factor):
+    scores = jnp.where(mask, nt(k, q) * factor, -1e30)
+    grown = jnp.exp(scores - jnp.max(scores, axis=0, keepdims=True))
+    return grown / jnp.sum(grown, axis=0, keepdims=True)
+
+
+def attend_forward(qkv, probs, mixed, block, line):
+    rows, width = mixed.shape
+    size = width // H
+    mask = line_mask(block, line)
+    factor = 1.0 / math.sqrt(size)
+
+    def body(b, _):
+        at = pl.ds(pl.multiple_of(b * block, block), block)
+        for h in range(H):
+            q, k, v = (qkv[at, n * width + h * size : n * width + (h + 1) * size] for n in range(3))
+            p = softmax_of(q, k, mask, factor)
+            probs[b * H + h] = p
+            mixed[at, h * size : (h + 1) * size] = tn(p.astype(BF16), v).astype(BF16)
+        return 0
+
+    lax.fori_loop(0, rows // block, body, 0)
+
+
+def attend_backward(qkv, probs, d_mixed, joined, block, line, keep):
+    rows, width = d_mixed.shape
+    size = width // H
+    mask = line_mask(block, line)
+    factor = 1.0 / math.sqrt(size)
+
+    def body(b, _):
+        at = pl.ds(pl.multiple_of(b * block, block), block)
+        for h in range(H):
+            q, k, v = (qkv[at, n * width + h * size : n * width + (h + 1) * size] for n in range(3))
+            p = probs[b * H + h] if keep else softmax_of(q, k, mask, factor)
+            dm = d_mixed[at, h * size : (h + 1) * size]
+            dp = nt(v, dm)
+            dv = nn(p.astype(BF16), dm).astype(BF16)
+            centre = jnp.sum(p * dp, axis=0, keepdims=True)
+            ds = (p * (dp - centre) * factor).astype(BF16)
+            joined[at, h * size : (h + 1) * size] = tn(ds, k).astype(BF16)
+            joined[at, width + h * size : width + (h + 1) * size] = nn(ds, q).astype(BF16)
+            joined[at, 2 * width + h * size : 2 * width + (h + 1) * size] = dv
+        return 0
+
+    lax.fori_loop(0, rows // block, body, 0)
+
+
+def norm_backward(a, c, rstd, gain, joined, w, dn):
+    width = a.shape[-1]
+    for j in range(3):
+        part = width // 3
+        dn[:, j * part : (j + 1) * part] = nt(joined[...], w[j * part : (j + 1) * part, :])
+    scaled = dn[...] * gain
+    mean = jnp.mean(scaled * a, axis=-1, keepdims=True)
+    return (c + rstd * (scaled - a * (rstd * rstd) * mean)).astype(BF16)
+
+
+def kernel(
+    nt_, ng, block_x, line_x, block_z, line_z,
+    tok, cot, gain_x, wx, ox, gain_z, wz, oz, px, pz, out,
+    tokr, cotr, outs, outr, mids, midr, cots, cotz, grads, gradr,
+    fwx, fox, fwz, foz, qkvx, qkvz, probs, mixed, dmix, joined, dn, ax, az,
+    tr_send, tr_recv, gz_send, gz_recv, w_send, w_recv, local,
+):
+    me, mine = lax.axis_index("tr"), lax.axis_index("gz")
+    sib, across = me + 1 - 2 * (me % 2), (me + 2) % nt_
+    half = mine % 2
+    partner = mine + 1 - 2 * half
+    rows, width = ax.shape
+
+    barrier = pltpu.get_barrier_semaphore()
+    for d in range(1, nt_):
+        pl.semaphore_signal(barrier, inc=1, device_id=((me + d) % nt_, mine), device_id_type=pl.DeviceIdType.MESH)
+    for d in range(1, ng):
+        pl.semaphore_signal(barrier, inc=1, device_id=(me, (mine + d) % ng), device_id_type=pl.DeviceIdType.MESH)
+    pl.semaphore_wait(barrier, nt_ + ng - 2)
+
+    def remote(src, dst, send, recv, t, g):
+        return pltpu.make_async_remote_copy(
+            src_ref=src, dst_ref=dst, send_sem=send, recv_sem=recv,
+            device_id=(t, g), device_id_type=pl.DeviceIdType.MESH,
+        )
+
+    def tr_copy(n, source, slots, d):
+        t = (me + d) % nt_
+        return remote(source(t), slots.at[me], tr_send.at[n, d], tr_recv.at[n, d], t, mine)
+
+    def gz_copy(n, source, slots, d):
+        g = (mine + d) % ng
+        return remote(source.at[g], slots.at[mine], gz_send.at[n, d], gz_recv.at[n, d], me, g)
+
+    far_first = [2, 3, 1] if nt_ == 4 else list(range(1, nt_))
+    gz_order = sorted(range(1, ng), key=lambda d: -min(d, ng - d))
+
+    owns = ((wx, ox), (wz, oz))
+    fulls = ((fwx, fox), (fwz, foz))
+
+    def piece(ref, t, h, mine_only):
+        depth = ref.shape[0] if mine_only else ref.shape[0] // nt_
+        cols = ref.shape[1] // 2
+        col = pl.ds(pl.multiple_of(h * cols, 128), cols)
+        row = pl.ds(0, depth) if mine_only else pl.ds(pl.multiple_of(t * depth, 16), depth)
+        return ref.at[row, col]
+
+    def own_copy(s, k, n, h, t):
+        return remote(
+            piece(owns[s][k], me, h, True), piece(fulls[s][k], me, h, False),
+            w_send.at[s, k, n], w_recv.at[s, k, me, h], t, mine,
+        )
+
+    def relay(s, k, n, h, t, g):
+        spot = piece(fulls[s][k], across, h, False)
+        return remote(spot, spot, w_send.at[s, k, n], w_recv.at[s, k, across, h], t, g)
+
+    def arrive(s, k, src, h):
+        spot = piece(fulls[s][k], src, h, False)
+        remote(spot, spot, w_send.at[s, k, 0], w_recv.at[s, k, src, h], sib, mine).wait_recv()
+
+    def weights_begin(s):
+        for k in range(2):
+            own_copy(s, k, 2, half, across).start()
+        for k in range(2):
+            own_copy(s, k, 0, 0, sib).start()
+            own_copy(s, k, 1, 1, sib).start()
+
+    def weights_relay(s):
+        for k in range(2):
+            arrive(s, k, across, half)
+            relay(s, k, 3, half, me, partner).start()
+            relay(s, k, 4, half, sib, mine).start()
+
+    def weights_end(s):
+        far = (sib + 2) % nt_
+        for k in range(2):
+            arrive(s, k, across, 1 - half)
+            relay(s, k, 5, 1 - half, sib, mine).start()
+        for k in range(2):
+            for h in range(2):
+                arrive(s, k, sib, h)
+                arrive(s, k, far, h)
+            own_copy(s, k, 0, 0, sib).wait_send()
+            own_copy(s, k, 1, 1, sib).wait_send()
+            own_copy(s, k, 2, half, across).wait_send()
+            relay(s, k, 3, half, me, partner).wait_send()
+            relay(s, k, 4, half, sib, mine).wait_send()
+            relay(s, k, 5, 1 - half, sib, mine).wait_send()
+
+    def wait_tr(n, source, slots):
+        for d in range(1, nt_):
+            tr_copy(n, source, slots, d).wait_send()
+            src = (me + nt_ - d) % nt_
+            remote(source(src), slots.at[src], tr_send.at[n, d], tr_recv.at[n, d], src, mine).wait_recv()
+
+    def wait_gz(n, source, slots):
+        for d in range(1, ng):
+            gz_copy(n, source, slots, d).wait_send()
+            src = (mine + ng - d) % ng
+            remote(source.at[src], slots.at[src], gz_send.at[n, d], gz_recv.at[n, d], me, src).wait_recv()
+
+    def from_tok(t):
+        return tok.at[:, t]
+
+    def from_cot(t):
+        return cot.at[:, t]
+
+    def from_out(t):
+        return outs.at[t]
+
+    for d in far_first:
+        tr_copy(0, from_tok, tokr, d).start()
+    weights_begin(0)
+    for d in far_first:
+        tr_copy(1, from_cot, cotr, d).start()
+    here = [pltpu.make_async_copy(tok.at[:, me], tokr.at[me], local.at[0]),
+            pltpu.make_async_copy(cot.at[:, me], cotr.at[me], local.at[1])]
+    n = 2
+    for s in range(2):
+        for k in range(2):
+            depth = owns[s][k].shape[0]
+            to = fulls[s][k].at[pl.ds(pl.multiple_of(me * depth, 16), depth)]
+            here.append(pltpu.make_async_copy(owns[s][k], to, local.at[n]))
+            n += 1
+    for copy in here:
+        copy.start()
+    for copy in here:
+        copy.wait()
+    wait_tr(0, from_tok, tokr)
+    ax[...] = nn(px[...], flat(tokr[...]).astype(BF16)).astype(BF16)
+
+    weights_relay(0)
+    weights_begin(1)
+    wait_tr(1, from_cot, cotr)
+    cot_lines = nn(px[...], flat(cotr[...]).astype(BF16))
+    cots[...] = cot_lines.reshape(cots.shape).astype(BF16)
+    cotz[mine] = cots[mine]
+    for d in gz_order:
+        gz_copy(1, cots, cotz, d).start()
+    weights_end(0)
+
+    rstd_x = project(ax[...].astype(F32), gain_x[...], fwx, qkvx)
+    attend_forward(qkvx, probs, mixed, block_x, line_x)
+    mid = ax[...].astype(F32) + nn(mixed[...], fox[...])
+    mids[...] = mid.reshape(mids.shape).astype(BF16)
+    for d in gz_order:
+        gz_copy(0, mids, midr, d).start()
+    midr[mine] = mids[mine]
+    weights_relay(1)
+    weights_end(1)
+
+    wait_gz(1, cots, cotz)
+    cz = nn(pz[...], flat(cotz[...]).astype(BF16))
+    dmix[...] = nt(cz.astype(BF16), foz[...]).astype(BF16)
+    wait_gz(0, mids, midr)
+    az[...] = nn(pz[...], flat(midr[...]).astype(BF16)).astype(BF16)
+    rstd_z = project(az[...].astype(F32), gain_z[...], fwz, qkvz)
+    attend_backward(qkvz, probs, dmix, joined, block_z, line_z, False)
+    cz = nn(pz[...], flat(cotz[...]).astype(BF16))
+    back = norm_backward(az[...].astype(F32), cz, rstd_z, gain_z[...], joined, fwz, dn)
+    grads[...] = tn(pz[...], back).reshape(grads.shape).astype(BF16)
+    for d in gz_order:
+        gz_copy(2, grads, gradr, d).start()
+    gradr[mine] = grads[mine]
+    wait_gz(2, grads, gradr)
+
+    dmix[...] = nt(flat(gradr[...]).astype(BF16), fox[...]).astype(BF16)
+    attend_backward(qkvx, probs, dmix, joined, block_x, line_x, True)
+    back = norm_backward(
+        ax[...].astype(F32), flat(gradr[...]), rstd_x, gain_x[...], joined, fwx, dn
+    )
+    outs[...] = tn(px[...], back).reshape(outs.shape).astype(BF16)
+    for d in far_first:
+        tr_copy(2, from_out, outr, d).start()
+    outr[me] = outs[me]
+    wait_tr(2, from_out, outr)
+    for t in range(nt_):
+        out[:, t] = outr[t]
+
+
+def one_hot(order):
+    return jnp.asarray(np.eye(len(order), dtype=np.float32)[order], BF16)
+
+
+def fits_kernel(trs, gzs, slab, y, x_own, width):
+    rows_own = y // trs
+    return trs == 4 and rows_own == gzs and (slab * trs * x_own) % 8 == 0 and (rows_own * x_own) % 16 == 0
+
+
+def fused(trs, gzs, tokens, cotangent, gain_x, wqkv_x, wo_x, gain_z, wqkv_z, wo_z):
+    slab, y, x_own, width = tokens.shape
+    y_own, x = y // trs, x_own * trs
+    rows, z = slab * y * x_own, slab * gzs
+    share = rows // gzs
+    index = np.arange(rows).reshape(trs, slab, y_own, x_own)
+    px = one_hot(index.transpose(2, 1, 0, 3).reshape(-1))
+    pz = one_hot(np.arange(rows).reshape(z, x).T.reshape(-1))
+    split = (slab, trs, y_own * x_own, width)
+    block_x, block_z = 80 if 80 % x == 0 else x, 80 if 80 % z == 0 else z
+    tr_slots, gz_slots = (trs, slab, y_own * x_own, width), (gzs, share, width)
+    vm = pl.BlockSpec(memory_space=pltpu.VMEM)
+    hbm = pl.BlockSpec(memory_space=pl.ANY)
+    wide = wqkv_x.shape[1]
+    result = pl.pallas_call(
+        functools.partial(kernel, trs, gzs, block_x, x, block_z, z),
+        out_shape=jax.ShapeDtypeStruct(split, BF16),
+        in_specs=[hbm, hbm, vm, hbm, hbm, vm, hbm, hbm, vm, vm],
+        out_specs=vm,
+        scratch_shapes=[pltpu.VMEM(tr_slots, BF16)] * 4
+        + [pltpu.VMEM(gz_slots, BF16)] * 6
+        + [pltpu.VMEM((width, wide), BF16), pltpu.VMEM((width, width), BF16)] * 2
+        + [pltpu.VMEM((rows, wide), BF16)] * 2
+        + [pltpu.VMEM((rows // block_x * H, block_x, block_x), F32)]
+        + [pltpu.VMEM((rows, width), BF16)] * 2
+        + [pltpu.VMEM((rows, wide), BF16), pltpu.VMEM((rows, width), F32)]
+        + [pltpu.VMEM((rows, width), BF16)] * 2
+        + [
+            pltpu.SemaphoreType.DMA((3, trs)),
+            pltpu.SemaphoreType.DMA((3, trs)),
+            pltpu.SemaphoreType.DMA((3, gzs)),
+            pltpu.SemaphoreType.DMA((3, gzs)),
+            pltpu.SemaphoreType.DMA((2, 2, 6)),
+            pltpu.SemaphoreType.DMA((2, 2, trs, 2)),
+            pltpu.SemaphoreType.DMA((6,)),
+        ],
+        compiler_params=pltpu.CompilerParams(
+            collective_id=0, has_side_effects=True, vmem_limit_bytes=56 * 1024 * 1024
+        ),
+    )(
+        tokens.reshape(split), cotangent.reshape(split),
+        gain_x.reshape(1, width), wqkv_x, wo_x, gain_z.reshape(1, width), wqkv_z, wo_z, px, pz,
+    )
+    return result.reshape(tokens.shape)
+
+
 def solution(mesh):
+    trs, gzs = mesh.shape["tr"], mesh.shape["gz"]
+
+    def body(tokens, *rest):
+        if fits_kernel(trs, gzs, *tokens.shape):
+            return fused(trs, gzs, tokens, *rest)
+        return per_device(tokens, *rest)
+
     return jax.shard_map(
-        per_device,
+        body,
         mesh=mesh,
         in_specs=(
             P("gz", None, "tr", None),

time: 195 us -> 117 us (0.60)
  Pallas kernels: 0 us -> 110 us
  waiting for transfers between devices: 75.3 us -> 0 us
  matrix products: 41.2 us -> 0 us
  blocking collectives: 30.5 us -> 0 us
  starting transfers between devices: 20.6 us -> 0 us
  between operations: 13.4 us -> 0.01 us
  local copies, waits for them, and re-layouts: 11.4 us -> 6.9 us
    pallas_call x0 -> x1, Pallas kernels: none -> 110 us  [fused(): pl.pallas_call(functools.partial(kernel, trs, gzs, block_x, x, block_z, z...]
    all_gather x4 -> x0, waiting for transfers between devices: 42.2 us -> none  [the longest x1 20.7 us: per_device(): lax.all_gather(wqkv_z, 'tr', axis=0, tiled=True)]
    dot_general x15 -> x0, matrix products: 36.8 us -> none  [the longest x2 7.38 us: backward(): d_normed = jnp.dot(joined, w_in.T, preferred_element_type=jnp.float32)]
    all_to_all x4 -> x0, waiting for transfers between devices: 30.5 us -> none  [the longest x1 13.1 us: per_device(): lax.all_to_all(cotangent, 'tr', split_axis=1, concat_axis=2, tiled=True)]
    all_to_all x2 -> x0, blocking collectives: 30.5 us -> none  [the longest x1 19.6 us: per_device(): lax.all_to_all(grad_columns, 'gz', split_axis=0, concat_axis=1, tiled=True)]
    all_to_all x4 -> x0, starting transfers between devices: 20.5 us -> none  [the longest x1 7.34 us: per_device(): lax.all_to_all(cot_lines.reshape(flat), 'gz', split_axis=1, concat_axis=0...]
    sub x2 -> x0, matrix products: 4.39 us -> none  [recompute(): expanded = jnp.exp(scores - highest)]
    reshape x4 -> x5, local copies, waits for them, and re-layouts: 3.37 us -> 6.89 us  [the longest x1 2.05 us: fused(): tokens.reshape(split)]
  transfers between devices with their start and end apart: 8 -> 0, of which waited for: 6 -> 0; matrix products, arithmetic and copies ran while one was open for 9% -> 0% of each run, Pallas kernels for 0% -> 0%
where the time goes in v2:
time: 117 us
  Pallas kernels  110 us (94%)
  local copies, waits for them, and re-layouts  6.9 us (6%)
    pallas_call x1, Pallas kernels, fused(): pl.pallas_call(functools.partial(kernel, trs, gzs, block_x, x, block_z, z...  110 us

profile of v2, /device:TPU:0, one launch (start us, length us, event | category | flops | bytes accessed | tf_op | source)
XLA Modules:
  0.0 116.5 jit_solution(4429001660865707463)
XLA Ops:
  0.0 0.0 copy-start.1
  0.0 1.3 %reshape.17.gain_x = f32[1,768]{1,0:T(1,128)} reshape(f32[768]{0:T(1024)} %param.12) | data formatting | bytes 6144 | tf_op jit(solution)/shard_map/reshape | solution.py:467
  1.3 0.0 copy-done.1
  1.3 0.6 reshape.18.gain_z
  1.9 0.0 copy-start
  1.9 2.0 %reshape.15.tok = bf16[5,4,16,768]{3,2,1,0:T(8,128)(2,1)} reshape(bf16[5,32,2,768]{3,2,1,0:T(2,128)(2,1)} %param.10) | data formatting | bytes 983040 | tf_op jit(solution)/shard_map/reshape | solution.py:466
  3.9 0.0 copy-done
  3.9 1.0 reshape.16.cot
  4.9 109.6 %shard_map.100 = bf16[5,4,16,768]{3,2,1,0:T(8,128)(2,1)} custom-call(bf16[5,4,16,768]{3,2,1,0:T(8,128)(2,1)} %reshape.15.tok, bf16[5,4,16,768]{3,2,1,0:T(8,128)(2,1)} %reshape.16.cot, f32[1,768]{1,0:T(1,128)} %reshape.17.gain_x, bf16[192,2304]{1,0:T(8,128)(2,1)} %wx.1, bf16[192,768]{1,0:T(8,128)(2,1)} %ox.1, f32[1,768]{1,0:T(1,128)} %reshape.18.gain_z, ...), custom_call_target="tpu_custom_call" | custom-call | tf_op jit(solution)/shard_map/pallas_call | solution.py:440
  114.5 2.0 %reshape.19 = bf16[5,32,2,768]{3,2,1,0:T(2,128)(2,1)} reshape(bf16[5,4,16,768]{3,2,1,0:T(8,128)(2,1)} %shard_map.100) | data formatting | bytes 983040 | tf_op jit(solution)/shard_map/reshape | solution.py:469
Async XLA Ops:
  0.0 1.3 %copy-start.1 = (f32[768]{0:T(1024)S(1)}, f32[768]{0:T(1024)}, u32[]{:S(2)}) copy-start(f32[768]{0:T(1024)} %param.15) | copy-start | bytes 9220
  1.9 2.1 %copy-start = (bf16[5,32,2,768]{3,2,1,0:T(2,128)(2,1)S(1)}, bf16[5,32,2,768]{3,2,1,0:T(2,128)(2,1)}, u32[]{:S(2)}) copy-start(bf16[5,32,2,768]{3,2,1,0:T(2,128)(2,1)} %param.11) | copy-start | bytes 1474564

commit v3 on v2

--- a/solution.py
+++ b/solution.py
@@ -270,49 +270,50 @@
     far_first = [2, 3, 1] if nt_ == 4 else list(range(1, nt_))
     gz_order = sorted(range(1, ng), key=lambda d: -min(d, ng - d))
 
-    owns = ((wx, ox), (wz, oz))
-    fulls = ((fwx, fox), (fwz, foz))
-
-    def piece(ref, t, h, mine_only):
+    owns = ((wx, wx, wx, ox), (wz, wz, wz, oz))
+    fulls = ((fwx, fwx, fwx, fox), (fwz, fwz, fwz, foz))
+
+    def piece(ref, k, t, h, mine_only):
         depth = ref.shape[0] if mine_only else ref.shape[0] // nt_
-        cols = ref.shape[1] // 2
-        col = pl.ds(pl.multiple_of(h * cols, 128), cols)
+        cols = width // 2
+        first = h * 3 + k if k < 3 else h
+        col = pl.ds(pl.multiple_of(first * cols, 128), cols)
         row = pl.ds(0, depth) if mine_only else pl.ds(pl.multiple_of(t * depth, 16), depth)
         return ref.at[row, col]
 
     def own_copy(s, k, n, h, t):
         return remote(
-            piece(owns[s][k], me, h, True), piece(fulls[s][k], me, h, False),
+            piece(owns[s][k], k, me, h, True), piece(fulls[s][k], k, me, h, False),
             w_send.at[s, k, n], w_recv.at[s, k, me, h], t, mine,
         )
 
     def relay(s, k, n, h, t, g):
-        spot = piece(fulls[s][k], across, h, False)
+        spot = piece(fulls[s][k], k, across, h, False)
         return remote(spot, spot, w_send.at[s, k, n], w_recv.at[s, k, across, h], t, g)
 
     def arrive(s, k, src, h):
-        spot = piece(fulls[s][k], src, h, False)
+        spot = piece(fulls[s][k], k, src, h, False)
         remote(spot, spot, w_send.at[s, k, 0], w_recv.at[s, k, src, h], sib, mine).wait_recv()
 
     def weights_begin(s):
-        for k in range(2):
+        for k in range(4):
             own_copy(s, k, 2, half, across).start()
-        for k in range(2):
+        for k in range(4):
             own_copy(s, k, 0, 0, sib).start()
             own_copy(s, k, 1, 1, sib).start()
 
     def weights_relay(s):
-        for k in range(2):
+        for k in range(4):
             arrive(s, k, across, half)
             relay(s, k, 3, half, me, partner).start()
             relay(s, k, 4, half, sib, mine).start()
 
     def weights_end(s):
         far = (sib + 2) % nt_
-        for k in range(2):
+        for k in range(4):
             arrive(s, k, across, 1 - half)
             relay(s, k, 5, 1 - half, sib, mine).start()
-        for k in range(2):
+        for k in range(4):
             for h in range(2):
                 arrive(s, k, sib, h)
                 arrive(s, k, far, h)
@@ -353,7 +354,7 @@
             pltpu.make_async_copy(cot.at[:, me], cotr.at[me], local.at[1])]
     n = 2
     for s in range(2):
-        for k in range(2):
+        for k in (0, 3):
             depth = owns[s][k].shape[0]
             to = fulls[s][k].at[pl.ds(pl.multiple_of(me * depth, 16), depth)]
             here.append(pltpu.make_async_copy(owns[s][k], to, local.at[n]))
@@ -455,8 +456,8 @@
             pltpu.SemaphoreType.DMA((3, trs)),
             pltpu.SemaphoreType.DMA((3, gzs)),
             pltpu.SemaphoreType.DMA((3, gzs)),
-            pltpu.SemaphoreType.DMA((2, 2, 6)),
-            pltpu.SemaphoreType.DMA((2, 2, trs, 2)),
+            pltpu.SemaphoreType.DMA((2, 4, 6)),
+            pltpu.SemaphoreType.DMA((2, 4, trs, 2)),
             pltpu.SemaphoreType.DMA((6,)),
         ],
         compiler_params=pltpu.CompilerParams(

time: 117 us -> 112 us (0.957)
  Pallas kernels: 110 us -> 104 us
    pallas_call x1, Pallas kernels: 110 us -> 104 us  [fused(): pl.pallas_call(functools.partial(kernel, trs, gzs, block_x, x, block_z, z...]
where the time goes in v3:
time: 112 us; the launch traced here: 111 us
  Pallas kernels  104 us (93%)
  local copies, waits for them, and re-layouts  6.9 us (6%)
    pallas_call x1, Pallas kernels, fused(): pl.pallas_call(functools.partial(kernel, trs, gzs, block_x, x, block_z, z...  104 us

profile of v3, /device:TPU:0, one launch (start us, length us, event | category | flops | bytes accessed | tf_op | source)
XLA Modules:
  0.0 111.4 jit_solution(13025423570718349214)
XLA Ops:
  0.0 0.0 copy-start.1
  0.0 1.3 %reshape.17.gain_x = f32[1,768]{1,0:T(1,128)} reshape(f32[768]{0:T(1024)} %param.12) | data formatting | bytes 6144 | tf_op jit(solution)/shard_map/reshape | solution.py:468
  1.3 0.0 copy-done.1
  1.3 0.6 reshape.18.gain_z
  1.9 0.0 copy-start
  1.9 2.0 %reshape.15.tok = bf16[5,4,16,768]{3,2,1,0:T(8,128)(2,1)} reshape(bf16[5,32,2,768]{3,2,1,0:T(2,128)(2,1)} %param.10) | data formatting | bytes 983040 | tf_op jit(solution)/shard_map/reshape | solution.py:467
  3.9 0.0 copy-done
  3.9 1.0 reshape.16.cot
  4.9 104.5 %shard_map.100 = bf16[5,4,16,768]{3,2,1,0:T(8,128)(2,1)} custom-call(bf16[5,4,16,768]{3,2,1,0:T(8,128)(2,1)} %reshape.15.tok, bf16[5,4,16,768]{3,2,1,0:T(8,128)(2,1)} %reshape.16.cot, f32[1,768]{1,0:T(1,128)} %reshape.17.gain_x, bf16[192,2304]{1,0:T(8,128)(2,1)} %wx.1, bf16[192,768]{1,0:T(8,128)(2,1)} %ox.1, f32[1,768]{1,0:T(1,128)} %reshape.18.gain_z, ...), custom_call_target="tpu_custom_call" | custom-call | tf_op jit(solution)/shard_map/pallas_call | solution.py:441
  109.4 2.0 %reshape.19 = bf16[5,32,2,768]{3,2,1,0:T(2,128)(2,1)} reshape(bf16[5,4,16,768]{3,2,1,0:T(8,128)(2,1)} %shard_map.100) | data formatting | bytes 983040 | tf_op jit(solution)/shard_map/reshape | solution.py:470
Async XLA Ops:
  0.0 1.3 %copy-start.1 = (f32[768]{0:T(1024)S(1)}, f32[768]{0:T(1024)}, u32[]{:S(2)}) copy-start(f32[768]{0:T(1024)} %param.15) | copy-start | bytes 9220
  1.9 2.1 %copy-start = (bf16[5,32,2,768]{3,2,1,0:T(2,128)(2,1)S(1)}, bf16[5,32,2,768]{3,2,1,0:T(2,128)(2,1)}, u32[]{:S(2)}) copy-start(bf16[5,32,2,768]{3,2,1,0:T(2,128)(2,1)} %param.11) | copy-start | bytes 1474564

commit v4 on v3

--- a/solution.py
+++ b/solution.py
@@ -175,12 +175,6 @@
     return key == query
 
 
-def softmax_of(q, k, mask, factor):
-    scores = jnp.where(mask, nt(k, q) * factor, -1e30)
-    grown = jnp.exp(scores - jnp.max(scores, axis=0, keepdims=True))
-    return grown / jnp.sum(grown, axis=0, keepdims=True)
-
-
 def attend_forward(qkv, probs, mixed, block, line):
     rows, width = mixed.shape
     size = width // H
@@ -189,11 +183,20 @@
 
     def body(b, _):
         at = pl.ds(pl.multiple_of(b * block, block), block)
-        for h in range(H):
-            q, k, v = (qkv[at, n * width + h * size : n * width + (h + 1) * size] for n in range(3))
-            p = softmax_of(q, k, mask, factor)
-            probs[b * H + h] = p
-            mixed[at, h * size : (h + 1) * size] = tn(p.astype(BF16), v).astype(BF16)
+        for first in range(0, H, 6):
+            heads = range(first, first + 6)
+            spans = [[pl.ds(n * width + h * size, size) for n in range(3)] for h in heads]
+            qk = [nt(qkv[at, sp[1]], qkv[at, sp[0]]) for sp in spans]
+            scores = [jnp.where(mask, x * factor, -1e30) for x in qk]
+            tops = [jnp.max(x, axis=0, keepdims=True) for x in scores]
+            grown = [jnp.exp(x - t) for x, t in zip(scores, tops)]
+            sums = [jnp.sum(x, axis=0, keepdims=True) for x in grown]
+            ps = [x / t for x, t in zip(grown, sums)]
+            for h, p in zip(heads, ps):
+                probs[b * H + h] = p
+            outs = [tn(p.astype(BF16), qkv[at, sp[2]]) for p, sp in zip(ps, spans)]
+            for sp, o in zip(spans, outs):
+                mixed[at, sp[0]] = o.astype(BF16)
         return 0
 
     lax.fori_loop(0, rows // block, body, 0)
@@ -207,17 +210,30 @@
 
     def body(b, _):
         at = pl.ds(pl.multiple_of(b * block, block), block)
-        for h in range(H):
-            q, k, v = (qkv[at, n * width + h * size : n * width + (h + 1) * size] for n in range(3))
-            p = probs[b * H + h] if keep else softmax_of(q, k, mask, factor)
-            dm = d_mixed[at, h * size : (h + 1) * size]
-            dp = nt(v, dm)
-            dv = nn(p.astype(BF16), dm).astype(BF16)
-            centre = jnp.sum(p * dp, axis=0, keepdims=True)
-            ds = (p * (dp - centre) * factor).astype(BF16)
-            joined[at, h * size : (h + 1) * size] = tn(ds, k).astype(BF16)
-            joined[at, width + h * size : width + (h + 1) * size] = nn(ds, q).astype(BF16)
-            joined[at, 2 * width + h * size : 2 * width + (h + 1) * size] = dv
+        for first in range(0, H, 6):
+            heads = range(first, first + 6)
+            spans = [[pl.ds(n * width + h * size, size) for n in range(3)] for h in heads]
+            dps = [nt(qkv[at, sp[2]], d_mixed[at, sp[0]]) for sp in spans]
+            if keep:
+                ps = [probs[b * H + h] for h in heads]
+            else:
+                qk = [nt(qkv[at, sp[1]], qkv[at, sp[0]]) for sp in spans]
+                scores = [jnp.where(mask, x * factor, -1e30) for x in qk]
+                tops = [jnp.max(x, axis=0, keepdims=True) for x in scores]
+                grown = [jnp.exp(x - t) for x, t in zip(scores, tops)]
+                sums = [jnp.sum(x, axis=0, keepdims=True) for x in grown]
+                ps = [x / t for x, t in zip(grown, sums)]
+            dvs = [nn(p.astype(BF16), d_mixed[at, sp[0]]) for p, sp in zip(ps, spans)]
+            centres = [jnp.sum(p * dp, axis=0, keepdims=True) for p, dp in zip(ps, dps)]
+            dss = [
+                (p * (dp - c) * factor).astype(BF16) for p, dp, c in zip(ps, dps, centres)
+            ]
+            dks = [nn(ds, qkv[at, sp[0]]) for ds, sp in zip(dss, spans)]
+            dqs = [tn(ds, qkv[at, sp[1]]) for ds, sp in zip(dss, spans)]
+            for sp, dq, dk, dv in zip(spans, dqs, dks, dvs):
+                joined[at, sp[0]] = dq.astype(BF16)
+                joined[at, sp[1]] = dk.astype(BF16)
+                joined[at, sp[2]] = dv.astype(BF16)
         return 0
 
     lax.fori_loop(0, rows // block, body, 0)
@@ -302,8 +318,8 @@
             own_copy(s, k, 0, 0, sib).start()
             own_copy(s, k, 1, 1, sib).start()
 
-    def weights_relay(s):
-        for k in range(4):
+    def weights_relay(s, pieces=range(4)):
+        for k in pieces:
             arrive(s, k, across, half)
             relay(s, k, 3, half, me, partner).start()
             relay(s, k, 4, half, sib, mine).start()
@@ -376,14 +392,15 @@
         gz_copy(1, cots, cotz, d).start()
     weights_end(0)
 
-    rstd_x = project(ax[...].astype(F32), gain_x[...], fwx, qkvx)
+    rstd_x = project(ax[...].astype(F32), gain_x[...][None], fwx, qkvx)
+    weights_relay(1, (0, 1))
     attend_forward(qkvx, probs, mixed, block_x, line_x)
+    weights_relay(1, (2, 3))
     mid = ax[...].astype(F32) + nn(mixed[...], fox[...])
     mids[...] = mid.reshape(mids.shape).astype(BF16)
     for d in gz_order:
         gz_copy(0, mids, midr, d).start()
     midr[mine] = mids[mine]
-    weights_relay(1)
     weights_end(1)
 
     wait_gz(1, cots, cotz)
@@ -391,10 +408,10 @@
     dmix[...] = nt(cz.astype(BF16), foz[...]).astype(BF16)
     wait_gz(0, mids, midr)
     az[...] = nn(pz[...], flat(midr[...]).astype(BF16)).astype(BF16)
-    rstd_z = project(az[...].astype(F32), gain_z[...], fwz, qkvz)
+    rstd_z = project(az[...].astype(F32), gain_z[...][None], fwz, qkvz)
     attend_backward(qkvz, probs, dmix, joined, block_z, line_z, False)
     cz = nn(pz[...], flat(cotz[...]).astype(BF16))
-    back = norm_backward(az[...].astype(F32), cz, rstd_z, gain_z[...], joined, fwz, dn)
+    back = norm_backward(az[...].astype(F32), cz, rstd_z, gain_z[...][None], joined, fwz, dn)
     grads[...] = tn(pz[...], back).reshape(grads.shape).astype(BF16)
     for d in gz_order:
         gz_copy(2, grads, gradr, d).start()
@@ -404,7 +421,7 @@
     dmix[...] = nt(flat(gradr[...]).astype(BF16), fox[...]).astype(BF16)
     attend_backward(qkvx, probs, dmix, joined, block_x, line_x, True)
     back = norm_backward(
-        ax[...].astype(F32), flat(gradr[...]), rstd_x, gain_x[...], joined, fwx, dn
+        ax[...].astype(F32), flat(gradr[...]), rstd_x, gain_x[...][None], joined, fwx, dn
     )
     outs[...] = tn(px[...], back).reshape(outs.shape).astype(BF16)
     for d in far_first:
@@ -465,7 +482,7 @@
         ),
     )(
         tokens.reshape(split), cotangent.reshape(split),
-        gain_x.reshape(1, width), wqkv_x, wo_x, gain_z.reshape(1, width), wqkv_z, wo_z, px, pz,
+        gain_x, wqkv_x, wo_x, gain_z, wqkv_z, wo_z, px, pz,
     )
     return result.reshape(tokens.shape)
 

time: 112 us -> 97.4 us (0.87)
  Pallas kernels: 104 us -> 91.5 us
  local copies, waits for them, and re-layouts: 6.9 us -> 5.01 us
    pallas_call x1, Pallas kernels: 104 us -> 91.5 us  [fused(): pl.pallas_call(functools.partial(kernel, trs, gzs, block_x, x, block_z, z...]
    reshape x2 -> x0, local copies, waits for them, and re-layouts: 1.89 us -> none  [the longest x1 1.3 us: fused(): gain_x.reshape(1, width)]
where the time goes in v4:
time: 97.4 us; the launch traced here: 96.5 us
  Pallas kernels  91.5 us (94%)
  local copies, waits for them, and re-layouts  5.01 us (5%)
    pallas_call x1, Pallas kernels, fused(): pl.pallas_call(functools.partial(kernel, trs, gzs, block_x, x, block_z, z...  91.5 us
    reshape x1, local copies, waits for them, and re-layouts, fused(): tokens.reshape(split)  2.05 us
    reshape x1, local copies, waits for them, and re-layouts, fused(): return result.reshape(tokens.shape)  1.99 us

profile of v4, /device:TPU:0, one launch (start us, length us, event | category | flops | bytes accessed | tf_op | source)
XLA Modules:
  0.0 96.5 jit_solution(9031747332429013384)
XLA Ops:
  0.0 0.0 copy-start
  0.0 2.0 %reshape.9.tok = bf16[5,4,16,768]{3,2,1,0:T(8,128)(2,1)} reshape(bf16[5,32,2,768]{3,2,1,0:T(2,128)(2,1)} %param.10) | data formatting | bytes 983040 | tf_op jit(solution)/shard_map/reshape | solution.py:484
  2.1 0.0 copy-done
  2.1 1.0 %reshape.10.cot = bf16[5,4,16,768]{3,2,1,0:T(8,128)(2,1)} reshape(bf16[5,32,2,768]{3,2,1,0:T(2,128)(2,1)S(1)} %copy-done) | data formatting | bytes 983040 | tf_op jit(solution)/shard_map/reshape | solution.py:484
  3.0 91.5 %shard_map.100 = bf16[5,4,16,768]{3,2,1,0:T(8,128)(2,1)} custom-call(bf16[5,4,16,768]{3,2,1,0:T(8,128)(2,1)} %reshape.9.tok, bf16[5,4,16,768]{3,2,1,0:T(8,128)(2,1)} %reshape.10.cot, f32[768]{0:T(1024)} %gain_x.1, bf16[192,2304]{1,0:T(8,128)(2,1)} %wx.1, bf16[192,768]{1,0:T(8,128)(2,1)} %ox.1, f32[768]{0:T(1024)} %gain_z.1, bf16[192,2304]{1,0:T(8,128)(2,1)} %wz.1, ...), custom_call_target="tpu_custom_call" | custom-call | tf_op jit(solution)/shard_map/pallas_call | solution.py:458
  94.6 2.0 %reshape.11 = bf16[5,32,2,768]{3,2,1,0:T(2,128)(2,1)} reshape(bf16[5,4,16,768]{3,2,1,0:T(8,128)(2,1)} %shard_map.100) | data formatting | bytes 983040 | tf_op jit(solution)/shard_map/reshape | solution.py:487
Async XLA Ops:
  0.0 2.1 %copy-start = (bf16[5,32,2,768]{3,2,1,0:T(2,128)(2,1)S(1)}, bf16[5,32,2,768]{3,2,1,0:T(2,128)(2,1)}, u32[]{:S(2)}) copy-start(bf16[5,32,2,768]{3,2,1,0:T(2,128)(2,1)} %param.11) | copy-start | bytes 1474564

commit v5 on v4

--- a/solution.py
+++ b/solution.py
@@ -190,8 +190,8 @@
             scores = [jnp.where(mask, x * factor, -1e30) for x in qk]
             tops = [jnp.max(x, axis=0, keepdims=True) for x in scores]
             grown = [jnp.exp(x - t) for x, t in zip(scores, tops)]
-            sums = [jnp.sum(x, axis=0, keepdims=True) for x in grown]
-            ps = [x / t for x, t in zip(grown, sums)]
+            sums = [1.0 / jnp.sum(x, axis=0, keepdims=True) for x in grown]
+            ps = [x * t for x, t in zip(grown, sums)]
             for h, p in zip(heads, ps):
                 probs[b * H + h] = p
             outs = [tn(p.astype(BF16), qkv[at, sp[2]]) for p, sp in zip(ps, spans)]
@@ -199,7 +199,7 @@
                 mixed[at, sp[0]] = o.astype(BF16)
         return 0
 
-    lax.fori_loop(0, rows // block, body, 0)
+    lax.fori_loop(0, rows // block, body, 0, unroll=True)
 
 
 def attend_backward(qkv, probs, d_mixed, joined, block, line, keep):
@@ -221,8 +221,8 @@
                 scores = [jnp.where(mask, x * factor, -1e30) for x in qk]
                 tops = [jnp.max(x, axis=0, keepdims=True) for x in scores]
                 grown = [jnp.exp(x - t) for x, t in zip(scores, tops)]
-                sums = [jnp.sum(x, axis=0, keepdims=True) for x in grown]
-                ps = [x / t for x, t in zip(grown, sums)]
+                sums = [1.0 / jnp.sum(x, axis=0, keepdims=True) for x in grown]
+                ps = [x * t for x, t in zip(grown, sums)]
             dvs = [nn(p.astype(BF16), d_mixed[at, sp[0]]) for p, sp in zip(ps, spans)]
             centres = [jnp.sum(p * dp, axis=0, keepdims=True) for p, dp in zip(ps, dps)]
             dss = [
@@ -236,7 +236,7 @@
                 joined[at, sp[2]] = dv.astype(BF16)
         return 0
 
-    lax.fori_loop(0, rows // block, body, 0)
+    lax.fori_loop(0, rows // block, body, 0, unroll=True)
 
 
 def norm_backward(a, c, rstd, gain, joined, w, dn):

time: 97.4 us -> 96 us (0.986)
  Pallas kernels: 91.5 us -> 90.1 us
    pallas_call x1, Pallas kernels: 91.5 us -> 90.1 us  [fused(): pl.pallas_call(functools.partial(kernel, trs, gzs, block_x, x, block_z, z...]
where the time goes in v5:
time: 96 us; the launch traced here: 95.2 us
  Pallas kernels  90.1 us (94%)
  local copies, waits for them, and re-layouts  5.01 us (5%)
    pallas_call x1, Pallas kernels, fused(): pl.pallas_call(functools.partial(kernel, trs, gzs, block_x, x, block_z, z...  90.1 us
    reshape x1, local copies, waits for them, and re-layouts, fused(): tokens.reshape(split)  2.05 us
    reshape x1, local copies, waits for them, and re-layouts, fused(): return result.reshape(tokens.shape)  1.99 us

profile of v5, /device:TPU:0, one launch (start us, length us, event | category | flops | bytes accessed | tf_op | source)
XLA Modules:
  0.0 95.2 jit_solution(3962409831156448853)
XLA Ops:
  0.0 0.0 copy-start
  0.0 2.0 %reshape.9.tok = bf16[5,4,16,768]{3,2,1,0:T(8,128)(2,1)} reshape(bf16[5,32,2,768]{3,2,1,0:T(2,128)(2,1)} %param.10) | data formatting | bytes 983040 | tf_op jit(solution)/shard_map/reshape | solution.py:484
  2.1 0.0 copy-done
  2.1 1.0 %reshape.10.cot = bf16[5,4,16,768]{3,2,1,0:T(8,128)(2,1)} reshape(bf16[5,32,2,768]{3,2,1,0:T(2,128)(2,1)S(1)} %copy-done) | data formatting | bytes 983040 | tf_op jit(solution)/shard_map/reshape | solution.py:484
  3.0 90.1 %shard_map.100 = bf16[5,4,16,768]{3,2,1,0:T(8,128)(2,1)} custom-call(bf16[5,4,16,768]{3,2,1,0:T(8,128)(2,1)} %reshape.9.tok, bf16[5,4,16,768]{3,2,1,0:T(8,128)(2,1)} %reshape.10.cot, f32[768]{0:T(1024)} %gain_x.1, bf16[192,2304]{1,0:T(8,128)(2,1)} %wx.1, bf16[192,768]{1,0:T(8,128)(2,1)} %ox.1, f32[768]{0:T(1024)} %gain_z.1, bf16[192,2304]{1,0:T(8,128)(2,1)} %wz.1, ...), custom_call_target="tpu_custom_call" | custom-call | tf_op jit(solution)/shard_map/pallas_call | solution.py:458
  93.2 2.0 %reshape.11 = bf16[5,32,2,768]{3,2,1,0:T(2,128)(2,1)} reshape(bf16[5,4,16,768]{3,2,1,0:T(8,128)(2,1)} %shard_map.100) | data formatting | bytes 983040 | tf_op jit(solution)/shard_map/reshape | solution.py:487
Async XLA Ops:
  0.0 2.1 %copy-start = (bf16[5,32,2,768]{3,2,1,0:T(2,128)(2,1)S(1)}, bf16[5,32,2,768]{3,2,1,0:T(2,128)(2,1)}, u32[]{:S(2)}) copy-start(bf16[5,32,2,768]{3,2,1,0:T(2,128)(2,1)} %param.11) | copy-start | bytes 1474564
